TPU v7x, 256 devices: a whole 4x4x8 slice. The times are simulated.
256 devices in a mesh: wide: 64 (over z, x_hi, y), narrow: 4 (over x_lo, core).
Axes of the slice: x: 4 (x_hi: 2, x_lo: 2; x = x_hi * 2 + x_lo), y: 4, z: 8, core: 2. Of those that a mesh axis runs over, the one named last changes fastest.
Arguments:
- feats: bfloat16 [131072, 128], P('wide'), may hold values from -6 to 6
- tiles: bfloat16 [16384, 256, 256], P(('wide', 'narrow')), may hold values from 0 to 2, as said below
- tile_rows: int32 [16384], P(('wide', 'narrow')), may hold values from 0 to 511, as said below
- tile_cols: int32 [16384], P(('wide', 'narrow')), may hold values from 0 to 511, as said below
- tile_count: int32 [256], P(('wide', 'narrow')), may hold values from 2 to 64, as said below
- weight: bfloat16 [128, 256], replicated, may hold values from -2 to 2
- cotangent: bfloat16 [131072, 256], P('wide'), may hold values from -6 to 6
Outputs:
- out: bfloat16 [131072, 256], P('wide')
- feats_grad: bfloat16 [131072, 128], P('wide')
- weight_grad: float32 [128, 256], replicated
Inputs may be any that keep to these rules, and one draw needn't show every extreme that they name: `tiles`: nonnegative edge weights. `tile_rows`: A slot's row block is one of the 8 row blocks of its device's wide index. `tile_cols`: A slot's column block belongs to a wide index at most 2 away from the slot's own wide index. `tile_count`: some device has all 64 slots live in every draw.
All inputs are finite; a program needn't handle non-finite values.
Results may differ from a plain program's by a relative error of at most 0.019.
Values may be sent and summed in bfloat16 or wider, within the bound.
No kernel may reach another device: no remote copies, remote signals or barrier semaphores. Data moves between devices by JAX's collectives and lax.ppermute only.
A program may use at most 128 MiB of HBM per device.

v0:
```python
import jax
import jax.numpy as jnp
from jax import lax
from jax.sharding import PartitionSpec as P

BLOCK = 256
REACH = 2


highest = lax.Precision.HIGHEST


def from_behind(x, axis, by):
    devices = lax.axis_size(axis)
    pairs = [(i, i + by) for i in range(devices) if 0 <= i + by < devices]
    return lax.ppermute(x, axis, pairs)


def per_device(feats, tiles, tile_rows, tile_cols, tile_count, weight, cotangent):
    slot_total = tiles.shape[0]
    node_rows, feature_width = feats.shape
    row_blocks = node_rows // BLOCK
    position = lax.axis_index("wide")
    window_count = (2 * REACH + 1) * row_blocks
    offsets = [offset for offset in range(-REACH, REACH + 1) if offset != 0]
    live_slots = jnp.arange(slot_total, dtype=jnp.int32) < tile_count[0]
    local_rows = tile_rows - position * row_blocks
    window_cols = tile_cols - (position - REACH) * row_blocks
    row_hot = (
        (local_rows[None, :] == jnp.arange(row_blocks, dtype=jnp.int32)[:, None])
        & live_slots[None, :]
    ).astype(jnp.float32)
    col_hot = (
        (window_cols[None, :] == jnp.arange(window_count, dtype=jnp.int32)[:, None])
        & live_slots[None, :]
    ).astype(jnp.float32)

    def over_slots(step_fn, initial):
        return step_fn(0, slot_total, initial)

    row_sums = jnp.sum(tiles, axis=2, dtype=jnp.float32)
    degree_part = jnp.dot(row_hot, row_sums, precision=highest)
    degree = 1.0 + lax.psum(degree_part, "narrow")
    inv_root = lax.rsqrt(degree).reshape(node_rows, 1)
    scaled = (inv_root * feats.astype(jnp.float32)).astype(jnp.bfloat16)
    neighbors = [from_behind(scaled, "wide", -offset) for offset in offsets]
    window = jnp.concatenate(neighbors[:REACH] + [scaled] + neighbors[REACH:], 0).reshape(
        window_count, BLOCK, feature_width
    )

    def forward_step(first_slot, slot_span, running):
        col_slabs = jnp.take(window, window_cols, axis=0)
        products = jnp.einsum("pij,pjf->pif", tiles, col_slabs, preferred_element_type=jnp.float32)
        return jnp.einsum("rp,pif->rif", row_hot, products, precision=highest)

    partial_value = over_slots(
        forward_step, jnp.zeros((row_blocks, BLOCK, feature_width), jnp.float32)
    )
    summed = lax.psum(
        partial_value.reshape(node_rows, feature_width).astype(jnp.bfloat16), "narrow"
    ).astype(jnp.float32)
    aggregate = (inv_root * (summed + scaled.astype(jnp.float32))).astype(jnp.bfloat16)
    out = jnp.dot(aggregate, weight, preferred_element_type=jnp.float32).astype(jnp.bfloat16)
    weight_term = jnp.dot(aggregate.T, cotangent, preferred_element_type=jnp.float32)
    weight_grad = lax.psum(weight_term, "wide")
    back_rows = jnp.dot(cotangent, weight.T, preferred_element_type=jnp.float32)
    back_scaled = (inv_root * back_rows).astype(jnp.bfloat16)
    back_blocks = back_scaled.reshape(row_blocks, BLOCK, feature_width)

    def backward_step(first_slot, slot_span, running):
        sources = jnp.take(back_blocks, local_rows, axis=0)
        products = jnp.einsum("pij,pif->pjf", tiles, sources, preferred_element_type=jnp.float32)
        return jnp.einsum("cp,pjf->cjf", col_hot, products, precision=highest)

    returned = over_slots(
        backward_step, jnp.zeros((window_count, BLOCK, feature_width), jnp.float32)
    )
    returned = returned.reshape(window_count * BLOCK, feature_width)
    rounded = returned.astype(jnp.bfloat16)
    received = lax.slice_in_dim(rounded, REACH * node_rows, (REACH + 1) * node_rows, axis=0).astype(
        jnp.float32
    )
    for offset in offsets:
        outgoing = lax.slice_in_dim(
            rounded, (offset + REACH) * node_rows, (offset + REACH + 1) * node_rows, axis=0
        )
        received = received + from_behind(outgoing, "wide", offset).astype(jnp.float32)
    received = lax.psum(received.astype(jnp.bfloat16), "narrow").astype(jnp.float32)
    feats_grad = (inv_root * (received + back_scaled.astype(jnp.float32))).astype(jnp.bfloat16)
    return (out, feats_grad, weight_grad)


def solution(mesh):
    placed = (
        P("wide", None),
        P(("wide", "narrow"), None, None),
        P(("wide", "narrow")),
        P(("wide", "narrow")),
        P(("wide", "narrow")),
        P(),
        P("wide", None),
    )
    return jax.shard_map(
        per_device,
        mesh=mesh,
        in_specs=placed,
        out_specs=(P("wide", None), P("wide", None), P()),
        check_vma=False,
    )
```

profile of v0, /device:TPU:2, one launch (start us, length us, event | category | flops | bytes accessed | tf_op | source)
XLA Modules:
  0.0 810.2 jit_solution(3551037021616598583)
XLA Ops:
  7.2 0.0 copy-start
  7.2 0.0 all-reduce.6.cloned.1.call-start
  8.0 5.7 convert_reduce_fusion
  13.7 0.1 fusion.30
  13.8 5.9 psum.28
  19.7 1.1 multiply_convert_fusion.2
  20.9 6.1 collective-permute-start
  26.9 3.4 collective-permute-start.1
  30.3 1.3 collective-permute-start.2
  31.6 1.3 collective-permute-start.3
  32.9 0.4 fusion.10
  33.4 3.1 gather_fusion.1
  36.4 9.7 %fusion.4 = f32[64,128,256]{2,1,0:T(8,128)} fusion(bf16[64,256,256]{2,1,0:T(8,128)(2,1)} %param.8, bf16[64,256,128]{2,1,0:T(8,128)(2,1)} %gather_fusion.1, pred[64]{0:T(512)(128)(4,1)S(1)} %get-tuple-element.5), kind=kOutput, calls=%fused_computation.7 | convolution fusion | flops 1075838976 | bytes 20971584 | tf_op jit(solution)/shard_map/pij,pif->pjf/dot_general | solution.py:72
  46.2 8.7 %copy.22 = f32[64,128,256]{1,0,2:T(8,128)} copy(f32[64,128,256]{2,1,0:T(8,128)} %fusion.4) | data formatting | bytes 16777216 | tf_op jit(solution)/shard_map/pij,pif->pjf/dot_general | solution.py:72
  54.9 7.4 fusion.13
  62.3 0.4 fusion.40
  62.7 0.9 copy.17
  63.6 1.3 collective-permute-start.4
  64.9 0.9 copy.18
  65.8 0.9 copy.19
  66.7 0.9 copy.20
  67.5 0.2 copy.16
  67.8 0.0 collective-permute-done
  67.8 1.3 collective-permute-start.5
  69.1 1.9 constant_dynamic-update-slice_fusion.4
  71.0 0.0 collective-permute-done.1
  71.0 6.0 collective-permute-start.6
  77.0 1.9 constant_dynamic-update-slice_fusion.3
  78.8 1.2 constant_dynamic-update-slice_fusion.2
  80.0 0.0 collective-permute-done.2
  80.0 7.4 collective-permute-start.7
  87.4 1.9 constant_dynamic-update-slice_fusion.1
  89.3 1.9 constant_dynamic-update-slice_fusion
  91.2 4.8 gather_fusion
  96.0 12.6 %fusion.6 = f32[64,128,256]{2,1,0:T(8,128)} fusion(bf16[64,256,256]{2,1,0:T(8,128)(2,1)} %param.8, bf16[64,256,128]{2,1,0:T(8,128)(2,1)} %gather_fusion, pred[64]{0:T(512)(128)(4,1)S(1)} %get-tuple-element.7), kind=kOutput, calls=%fused_computation.9 | convolution fusion | flops 1075838976 | bytes 20971584 | tf_op jit(solution)/shard_map/pij,pjf->pif/dot_general | solution.py:53
  108.6 8.7 %copy.21 = f32[64,128,256]{1,0,2:T(8,128)} copy(f32[64,128,256]{2,1,0:T(8,128)} %fusion.6) | data formatting | bytes 16777216 | tf_op jit(solution)/shard_map/pij,pjf->pif/dot_general | solution.py:53
  117.3 6.2 fusion.16
  123.4 0.9 copy.15
  124.3 2.6 fusion.22
  127.0 0.0 all-reduce.6.cloned.1.call-update
  127.0 0.0 all-reduce.4.cloned.1.call-start
  127.1 55.6 %all-reduce.6.cloned.1.call-done = (bf16[2048,128]{1,0:T(8,128)(2,1)}, bf16[2048,128]{1,0:T(8,128)(2,1)}) async-done(((bf16[2048,128]{1,0:T(8,128)(2,1)}, bf16[2048,128]{1,0:T(8,128)(2,1)}), (bf16[2048,128]{1,0:T(8,128)(2,1)}, bf16[2048,128]{1,0:T(8,128)(2,1)})) %all-reduce.6.cloned.1.call-update) | async-done | bytes 1048592 | tf_op jit(solution)/shard_map/psum | solution.py:59
  182.7 2.2 multiply_convert_fusion
  184.9 2.6 fusion.39
  187.5 0.0 all-reduce.4.cloned.1.call-update
  187.6 1.7 convolution_convert_fusion
  189.3 612.5 %all-reduce.4.cloned.1.call-done = f32[128,256]{1,0:T(8,128)} async-done(((f32[128,256]{1,0:T(8,128)}), f32[128,256]{1,0:T(8,128)}) %all-reduce.4.cloned.1.call-update) | async-done | bytes 131088 | tf_op jit(solution)/shard_map/psum | solution.py:65
  801.8 1.6 copy.32
  (24 shorter events, 0.1 us)
Async XLA Ops:
  7.2 25.7 %copy-start = (bf16[2048,256]{1,0:T(8,128)(2,1)S(1)}, bf16[2048,256]{1,0:T(8,128)(2,1)}, u32[]{:S(2)}) copy-start(bf16[2048,256]{1,0:T(8,128)(2,1)} %param.13) | copy-start | bytes 3145732
  7.2 175.5 %all-reduce.6.cloned.1.call-start = ((), (), s32[]{:S(2)}) async-start(), calls=%async_computation.1 | async-start | bytes 2097152 | tf_op jit(solution)/shard_map/psum | solution.py:59
  8.0 5.7 copy-start.4
  8.0 11.8 %copy-start.1 = (bf16[2048,128]{1,0:T(8,128)(2,1)S(1)}, bf16[2048,128]{1,0:T(8,128)(2,1)}, u32[]{:S(2)}) copy-start(bf16[2048,128]{1,0:T(8,128)(2,1)} %param.7) | copy-start | bytes 1572868
  8.0 24.9 %copy-start.3 = (bf16[128,256]{1,0:T(8,128)(2,1)S(1)}, bf16[128,256]{1,0:T(8,128)(2,1)}, u32[]{:S(2)}) copy-start(bf16[128,256]{1,0:T(8,128)(2,1)} %param.12) | copy-start | bytes 196612
  20.9 46.9 %collective-permute-start = (bf16[2048,128]{1,0:T(8,128)(2,1)}, bf16[2048,128]{1,0:T(8,128)(2,1)}, u32[]{:S(2)}, u32[]{:S(2)}) collective-permute-start(bf16[2048,128]{1,0:T(8,128)(2,1)} %multiply_convert_fusion.2), channel_id=1, source_target_pairs={{0,8},{4,12},{8,16},{12,20},{16,24},{20,28},{24,32},{28,36},{32,40... | collective-permute-start | bytes 1572872 | tf_op jit(solution)/shard_map/ppermute | solution.py:16
  26.9 44.0 %collective-permute-start.1 = (bf16[2048,128]{1,0:T(8,128)(2,1)}, bf16[2048,128]{1,0:T(8,128)(2,1)}, u32[]{:S(2)}, u32[]{:S(2)}) collective-permute-start(bf16[2048,128]{1,0:T(8,128)(2,1)} %multiply_convert_fusion.2), channel_id=1, source_target_pairs={{0,4},{4,8},{8,12},{12,16},{16,20},{20,24},{24,28},{28,32},{32,36}... | collective-permute-start | bytes 1572872 | tf_op jit(solution)/shard_map/ppermute | solution.py:16
  30.3 49.7 %collective-permute-start.2 = (bf16[2048,128]{1,0:T(8,128)(2,1)}, bf16[2048,128]{1,0:T(8,128)(2,1)}, u32[]{:S(2)}, u32[]{:S(2)}) collective-permute-start(bf16[2048,128]{1,0:T(8,128)(2,1)} %multiply_convert_fusion.2), channel_id=1, source_target_pairs={{4,0},{8,4},{12,8},{16,12},{20,16},{24,20},{28,24},{32,28},{36,32}... | collective-permute-start | bytes 1572872 | tf_op jit(solution)/shard_map/ppermute | solution.py:16
  31.6 57.8 %collective-permute-start.3 = (bf16[2048,128]{1,0:T(8,128)(2,1)}, bf16[2048,128]{1,0:T(8,128)(2,1)}, u32[]{:S(2)}, u32[]{:S(2)}) collective-permute-start(bf16[2048,128]{1,0:T(8,128)(2,1)} %multiply_convert_fusion.2), channel_id=1, source_target_pairs={{8,0},{12,4},{16,8},{20,12},{24,16},{28,20},{32,24},{36,28},{40,32... | collective-permute-start | bytes 1572872 | tf_op jit(solution)/shard_map/ppermute | solution.py:16
  46.2 8.7 %copy-start.5 = (s32[64]{0:T(128)S(1)}, s32[64]{0:T(128)}, u32[]{:S(2)}) copy-start(s32[64]{0:T(128)} %param.10) | copy-start | bytes 772
  63.6 60.7 %collective-permute-start.4 = (bf16[2048,128]{1,0:T(8,128)(2,1)}, bf16[2048,128]{1,0:T(8,128)(2,1)}, u32[]{:S(2)}, u32[]{:S(2)}) collective-permute-start(bf16[2048,128]{1,0:T(8,128)(2,1)} %bitcast.9), channel_id=1, source_target_pairs={{8,0},{12,4},{16,8},{20,12},{24,16},{28,20},{32,24},{36,28},{40,32... | collective-permute-start | bytes 1572872 | tf_op jit(solution)/shard_map/ppermute | solution.py:16
  67.8 56.5 %collective-permute-start.5 = (bf16[2048,128]{1,0:T(8,128)(2,1)}, bf16[2048,128]{1,0:T(8,128)(2,1)}, u32[]{:S(2)}, u32[]{:S(2)}) collective-permute-start(bf16[2048,128]{1,0:T(8,128)(2,1)} %bitcast.10), channel_id=1, source_target_pairs={{4,0},{8,4},{12,8},{16,12},{20,16},{24,20},{28,24},{32,28},{36,32}... | collective-permute-start | bytes 1572872 | tf_op jit(solution)/shard_map/ppermute | solution.py:16
  71.0 53.4 %collective-permute-start.6 = (bf16[2048,128]{1,0:T(8,128)(2,1)}, bf16[2048,128]{1,0:T(8,128)(2,1)}, u32[]{:S(2)}, u32[]{:S(2)}) collective-permute-start(bf16[2048,128]{1,0:T(8,128)(2,1)} %bitcast.11), channel_id=1, source_target_pairs={{0,4},{4,8},{8,12},{12,16},{16,20},{20,24},{24,28},{28,32},{32,36}... | collective-permute-start | bytes 1572872 | tf_op jit(solution)/shard_map/ppermute | solution.py:16
  80.0 44.3 %collective-permute-start.7 = (bf16[2048,128]{1,0:T(8,128)(2,1)}, bf16[2048,128]{1,0:T(8,128)(2,1)}, u32[]{:S(2)}, u32[]{:S(2)}) collective-permute-start(bf16[2048,128]{1,0:T(8,128)(2,1)} %bitcast.12), channel_id=1, source_target_pairs={{0,8},{4,12},{8,16},{12,20},{16,24},{20,28},{24,32},{28,36},{32,40... | collective-permute-start | bytes 1572872 | tf_op jit(solution)/shard_map/ppermute | solution.py:16
  127.0 674.8 %all-reduce.4.cloned.1.call-start = ((), (), s32[]{:S(2)}) async-start(), calls=%async_computation | async-start | bytes 262144 | tf_op jit(solution)/shard_map/psum | solution.py:65
  182.7 4.9 copy-start.2
Sparse Core Ops, SparseCore 0:
  127.1 55.4 all-reduce.5
  187.7 614.0 all-reduce.3
where the time goes:
time: 811 us; the launch traced here: 810 us
  waiting for transfers between devices  668 us (82%)
  matrix products  40.8 us (5%)
  local copies, waits for them, and re-layouts  39 us (5%)
  starting transfers between devices  28.1 us (3%)
  between operations  15 us (2%)
  other arithmetic  13.3 us (2%)
    psum x1, waiting for transfers between devices, per_device(): weight_grad = lax.psum(weight_term, 'wide')  612 us
    psum x1, waiting for transfers between devices, per_device(): lax.psum(partial_value.reshape(node_rows, feature_width).astype(jnp.bfloa...  55.6 us
    ppermute x8, starting transfers between devices, from_behind(): return lax.ppermute(x, axis, pairs)  28 us
  transfers between devices with their start and end apart: 10, of which 2 were waited for; matrix products, arithmetic and copies ran while one was open for 10% of the time, Pallas kernels for 0%

commit v1 on v0

v1 whole, which is shorter than its diff:
```python
import jax
import jax.numpy as jnp
from jax import lax
from jax.experimental import pallas as pl
from jax.experimental.pallas import tpu as pltpu
from jax.sharding import PartitionSpec as P

BLOCK = 256
REACH = 2
STEP = 8
OFFSETS = (-2, -1, 1, 2)
f32 = jnp.float32
bf16 = jnp.bfloat16
VMEM = pl.BlockSpec(memory_space=pltpu.VMEM)
SMEM = pl.BlockSpec(memory_space=pltpu.SMEM)
LIMIT = pltpu.CompilerParams(vmem_limit_bytes=32 * 2**20)

NT = (((1,), (1,)), ((), ()))
TN = (((0,), (0,)), ((), ()))


def shape(dims, dtype):
    return jax.ShapeDtypeStruct(dims, dtype)


def call(kernel, ins, outs, scratch=(), name=None):
    return pl.pallas_call(
        kernel,
        in_specs=ins,
        out_specs=[VMEM] * len(outs),
        out_shape=outs,
        scratch_shapes=list(scratch),
        compiler_params=LIMIT,
        name=name,
    )


def each_step(count, step_fn):
    def body(step, carry):
        step_fn(step * STEP)
        return carry

    lax.fori_loop(0, (count + STEP - 1) // STEP, body, 0)


def turn_kernel(feats_ref, out_ref):
    for block in range(out_ref.shape[0]):
        out_ref[block] = feats_ref[block].T


def degree_kernel(count_ref, rows_ref, tiles_ref, out_ref, total):
    blocks = out_ref.shape[0]
    count = count_ref[0]
    total[...] = jnp.zeros_like(total)
    ones = jnp.ones((8, BLOCK), bf16)

    def step_fn(first):
        sums = [
            lax.dot_general(ones, tiles_ref[first + k], NT, preferred_element_type=f32)
            for k in range(STEP)
        ]
        for k in range(STEP):
            row = jnp.where(first + k < count, rows_ref[first + k], blocks)
            total[row] += sums[k]

    each_step(count, step_fn)
    for block in range(blocks):
        out_ref[block : block + 1] = total[block, 0:1]


def backward_kernel(
    count_ref, rows_ref, slots_ref, tiles_ref, weight_ref, cot_ref, inv_ref,
    back_ref, own_ref, keep_ref, send_ref, total,
):
    blocks = cot_ref.shape[0]
    count = count_ref[0]
    for block in range(blocks):
        rows = lax.dot_general(weight_ref[...], cot_ref[block], NT, preferred_element_type=f32)
        back_ref[block] = (rows * inv_ref[block : block + 1]).astype(bf16)
    total[...] = jnp.zeros_like(total)

    def step_fn(first):
        products = [
            jnp.dot(back_ref[rows_ref[first + k]], tiles_ref[first + k], preferred_element_type=f32)
            for k in range(STEP)
        ]
        for k in range(STEP):
            slot = jnp.where(first + k < count, slots_ref[first + k], 5 * blocks)
            total[slot] += products[k]

    each_step(count, step_fn)
    for part, (ref, at) in enumerate(
        ((own_ref, None), (keep_ref, 0), (send_ref, 0), (keep_ref, 1), (send_ref, 1))
    ):
        for block in range(blocks):
            value = total[part * blocks + block].astype(bf16)
            if at is None:
                ref[block] = value
            else:
                ref[at, block] = value


def forward_kernel(
    place_ref, count_ref, rows_ref, slots_ref, tiles_ref, own_ref, x0, x1, x2, x3, inv_ref, invs_ref,
    keep_ref, send_ref, window, total,
):
    blocks = own_ref.shape[0]
    quarter = own_ref.shape[1] // 4
    count = count_ref[0]
    me = place_ref[0]
    for block in range(blocks):
        window[block] = (own_ref[block].astype(f32) * inv_ref[block : block + 1]).astype(bf16)
    for part, ref in enumerate((x0, x1, x2, x3)):
        who = me ^ part
        for block in range(blocks):
            scale = invs_ref[who, block : block + 1]
            window[(part + 1) * blocks + block] = (ref[block].astype(f32) * scale).astype(bf16)
    total[...] = jnp.zeros_like(total)

    def step_fn(first):
        products = [
            lax.dot_general(
                window[slots_ref[first + k]], tiles_ref[first + k], NT, preferred_element_type=f32
            )
            for k in range(STEP)
        ]
        for k in range(STEP):
            row = jnp.where(first + k < count, rows_ref[first + k], blocks)
            total[row] += products[k]

    each_step(count, step_fn)
    for ref, at, part in ((keep_ref, 0, 0), (send_ref, 0, 1), (keep_ref, 1, 2), (send_ref, 1, 3)):
        start = pl.multiple_of((me ^ part) * quarter, quarter)
        for block in range(blocks):
            ref[at, block] = total[block, pl.ds(start, quarter)].astype(bf16)


def aggregate_kernel(place_ref, mine_ref, other_ref, inv_ref, feats_ref, cot_ref, agg_ref, term_ref):
    blocks = mine_ref.shape[0]
    quarter = mine_ref.shape[1]
    start = pl.multiple_of(place_ref[0] * quarter, quarter)
    term = jnp.zeros(term_ref.shape, f32)
    for block in range(blocks):
        inv = inv_ref[block : block + 1]
        own = (feats_ref[block, pl.ds(start, quarter)].astype(f32) * inv).astype(bf16)
        summed = mine_ref[block].astype(f32) + other_ref[block].astype(f32)
        agg = (inv * (summed + own.astype(f32))).astype(bf16)
        agg_ref[block] = agg
        term = term + jnp.dot(agg, cot_ref[block], preferred_element_type=f32)
    term_ref[...] = term.astype(bf16)


def out_kernel(agg_ref, weight_ref, out_ref):
    parts, blocks, quarter, _ = agg_ref.shape
    for block in range(blocks):
        total = None
        for part in range(parts):
            product = lax.dot_general(
                agg_ref[part, block],
                weight_ref[part * quarter : (part + 1) * quarter],
                TN,
                preferred_element_type=f32,
            )
            total = product if total is None else total + product
        out_ref[block] = total.astype(bf16)


def grad_kernel(place_ref, mine_ref, other_ref, back_ref, inv_ref, out_ref):
    first = place_ref[0] * 2
    for k in range(2):
        inv = inv_ref[pl.ds(first + k, 1)]
        summed = mine_ref[k].astype(f32) + other_ref[k].astype(f32)
        grad = inv * (summed + back_ref[first + k].astype(f32))
        out_ref[k] = grad.T.astype(bf16)


def per_device(feats, tiles, tile_rows, tile_cols, tile_count, weight, cotangent):
    nodes, width = feats.shape
    hidden = cotangent.shape[1]
    blocks = nodes // BLOCK
    quarter = width // 4
    wides = lax.axis_size("wide")
    narrows = lax.axis_size("narrow")
    wide = lax.axis_index("wide")
    me = lax.axis_index("narrow").astype(jnp.int32)
    place = me.reshape(1)

    def swap(x, by):
        return lax.ppermute(x, "narrow", [(i, i ^ by) for i in range(narrows)])

    def fetch(x, sign):
        pairs = [
            (w * narrows + n, (w + sign * OFFSETS[n]) * narrows + n)
            for w in range(wides)
            for n in range(narrows)
            if 0 <= w + sign * OFFSETS[n] < wides
        ]
        return lax.ppermute(x, ("wide", "narrow"), pairs)

    rows = tile_rows - wide * blocks
    offset = tile_cols // blocks - wide
    owner = jnp.where(offset < 0, offset + 2, offset + 1)
    part = jnp.where(offset == 0, 0, 1 + (owner ^ me))
    slots = part * blocks + tile_cols % blocks

    (feats_t,) = call(turn_kernel, [VMEM], [shape((blocks, width, BLOCK), bf16)], name="turn")(
        feats.reshape(blocks, BLOCK, width)
    )
    x0 = fetch(feats_t, -1)

    (degree_part,) = call(
        degree_kernel,
        [SMEM, SMEM, VMEM],
        [shape((blocks, BLOCK), f32)],
        [pltpu.VMEM((blocks + 1, 8, BLOCK), f32)],
        name="degree",
    )(tile_count, rows, tiles)
    degree = 1.0 + jnp.sum(lax.all_gather(degree_part, "narrow"), axis=0)
    inv = lax.rsqrt(degree)
    inv_far = fetch(inv, -1)

    cot = cotangent.reshape(blocks, BLOCK, hidden)
    block_shape = (blocks, width, BLOCK)
    back, q_own, q_keep, q_send = call(
        backward_kernel,
        [SMEM] * 3 + [VMEM] * 4,
        [
            shape(block_shape, bf16),
            shape(block_shape, bf16),
            shape((2,) + block_shape, bf16),
            shape((2,) + block_shape, bf16),
        ],
        [pltpu.VMEM((5 * blocks + 1, width, BLOCK), f32)],
        name="backward",
    )(tile_count, rows, slots, tiles, weight, cot, inv)
    q_half = q_keep.astype(f32) + swap(q_send, 1).astype(f32)
    q_whole = q_half[0] + swap(q_half[1].astype(bf16), 2).astype(f32)
    q_far = fetch(q_whole.astype(bf16), 1)

    x1 = swap(x0, 1)
    x2 = swap(x0, 2)
    x3 = swap(x2, 1)
    invs = lax.all_gather(inv_far, "narrow")
    p_keep, p_send = call(
        forward_kernel,
        [SMEM] * 4 + [VMEM] * 8,
        [shape((2, blocks, quarter, BLOCK), bf16)] * 2,
        [
            pltpu.VMEM((5 * blocks, width, BLOCK), bf16),
            pltpu.VMEM((blocks + 1, width, BLOCK), f32),
        ],
        name="forward",
    )(place, tile_count, rows, slots, tiles, feats_t, x0, x1, x2, x3, inv, invs)
    p_half = p_keep.astype(f32) + swap(p_send, 1).astype(f32)
    p_other = swap(p_half[1].astype(bf16), 2)
    agg, term = call(
        aggregate_kernel,
        [SMEM] + [VMEM] * 5,
        [shape((blocks, quarter, BLOCK), bf16), shape((quarter, hidden), bf16)],
        name="aggregate",
    )(place, p_half[0], p_other, inv, feats_t, cot)

    terms = jnp.broadcast_to(term[None], (wides, quarter, hidden))
    terms = lax.all_to_all(terms, "wide", 0, 0)
    weight_part = jnp.sum(terms.astype(f32), axis=0)
    weight_grad = lax.all_gather(weight_part, "narrow", tiled=True)

    agg_all = lax.all_gather(agg, "narrow")
    (out,) = call(out_kernel, [VMEM] * 2, [shape((blocks, BLOCK, hidden), bf16)], name="out")(
        agg_all, weight
    )

    z = (q_own.astype(f32) + q_far.astype(f32)).reshape(narrows, 2, width, BLOCK)

    def piece(by):
        return lax.dynamic_index_in_dim(z, me ^ by, 0, keepdims=False)

    z_got = swap(jnp.stack([piece(1), piece(3)]).astype(bf16), 1).astype(f32)
    z_mine = piece(0) + z_got[0]
    z_other = swap((piece(2) + z_got[1]).astype(bf16), 2)
    (grad,) = call(
        grad_kernel, [SMEM] + [VMEM] * 4, [shape((2, BLOCK, width), bf16)], name="grad"
    )(place, z_mine, z_other, back, inv)
    feats_grad = lax.all_gather(grad, "narrow", tiled=True)
    return (out.reshape(nodes, hidden), feats_grad.reshape(nodes, width), weight_grad)


def solution(mesh):
    placed = (
        P("wide", None),
        P(("wide", "narrow"), None, None),
        P(("wide", "narrow")),
        P(("wide", "narrow")),
        P(("wide", "narrow")),
        P(),
        P("wide", None),
    )
    return jax.shard_map(
        per_device,
        mesh=mesh,
        in_specs=placed,
        out_specs=(P("wide", None), P("wide", None), P()),
        check_vma=False,
    )
```

time: 811 us -> 159 us (0.20)
  the two profiles are of different devices: /device:TPU:2 before, /device:TPU:35 now
where the time goes in v1:
time: 159 us; the launch traced here: 158 us
  waiting for transfers between devices  60.4 us (38%)
  starting transfers between devices  39 us (25%)
  blocking collectives  37.7 us (24%)
  local copies, waits for them, and re-layouts  7.94 us (5%)
  Pallas kernels  7.24 us (5%)
  other arithmetic  3.96 us (2%)
    ppermute x3, waiting for transfers between devices, fetch(): return lax.ppermute(x, ('wide', 'narrow'), pairs)  33.6 us
    ppermute x9, waiting for transfers between devices, swap(): return lax.ppermute(x, 'narrow', [(i, i ^ by) for i in range(narrows)])  26.8 us
    ppermute x9, starting transfers between devices, swap(): return lax.ppermute(x, 'narrow', [(i, i ^ by) for i in range(narrows)])  17.8 us
    ppermute x3, starting transfers between devices, fetch(): return lax.ppermute(x, ('wide', 'narrow'), pairs)  12.4 us
    all_gather x1, blocking collectives, per_device(): agg_all = lax.all_gather(agg, 'narrow')  9.41 us
    all_gather x1, blocking collectives, per_device(): invs = lax.all_gather(inv_far, 'narrow')  9.25 us
    all_to_all x1, starting transfers between devices, per_device(): terms = lax.all_to_all(terms, 'wide', 0, 0)  8.7 us
    all_gather x1, blocking collectives, per_device(): feats_grad = lax.all_gather(grad, 'narrow', tiled=True)  7.29 us
  transfers between devices with their start and end apart: 13, of which 5 were waited for; matrix products, arithmetic and copies ran while one was open for 3% of the time, Pallas kernels for 3%

profile of v1, /device:TPU:35, one launch (start us, length us, event | category | flops | bytes accessed | tf_op | source)
XLA Modules:
  0.0 157.8 jit_solution(3383319104558040451)
XLA Ops:
  0.6 1.0 copy-done.2
  1.7 0.2 turn.1.own_ref.feats_ref
  1.9 5.9 %collective-permute-start = (bf16[8,128,256]{2,1,0:T(8,128)(2,1)S(1)}, bf16[8,128,256]{2,1,0:T(8,128)(2,1)S(1)}, u32[]{:S(2)}, u32[]{:S(2)}) collective-permute-start(bf16[8,128,256]{2,1,0:T(8,128)(2,1)S(1)} %turn.1.own_ref.feats_ref), channel_id=1, source_target_pairs={{0,8},{1,5},{4,12},{5,9},{6,2},{8,16},{9,13},{10,6},{11,3},{12,20}... | collective-permute-start | bytes 1572872 | tf_op jit(solution)/shard_map/ppermute | solution.py:198
  8.5 0.7 broadcast_subtract_fusion.rows_ref
  9.1 3.4 %copy-done = bf16[64,256,256]{2,1,0:T(8,128)(2,1)S(1)} copy-done((bf16[64,256,256]{2,1,0:T(8,128)(2,1)S(1)}, bf16[64,256,256]{2,1,0:T(8,128)(2,1)}, u32[]{:S(2)}) %copy-start) | copy-done | bytes 8388632
  12.5 0.9 degree.1
  13.5 6.3 %all-gather = f32[32,256]{1,0:T(8,128)S(1)} all-gather(f32[8,256]{1,0:T(8,128)S(1)} %degree.1), channel_id=2, replica_groups=mesh['wide'=64,'narrow'=4] {'narrow'}, dimensions={0}, use_global_device_ids=true | all-gather | bytes 40960 | tf_op jit(solution)/shard_map/all_gather | solution.py:218
  19.8 0.0 slice-start.1
  19.8 1.9 %backward.1 = (bf16[8,128,256]{2,1,0:T(8,128)(2,1)S(1)}, bf16[8,128,256]{2,1,0:T(8,128)(2,1)S(1)}, bf16[2,8,128,256]{3,2,1,0:T(8,128)(2,1)S(1)}, bf16[2,8,128,256]{3,2,1,0:T(8,128)(2,1)S(1)}) custom-call(s32[1]{0:T(128)S(6)} %copy.12.count_ref, s32[64]{0:T(128)S(1)} %broadcast_subtract_fusion.rows_ref, s32[64]{0:T(128)S(1)} %fusion.7.slots_ref, ...), custom_call_target="tpu_custom_call" | custom-call | tf_op jit(solution)/shard_map/backward/pallas_call | solution.py:224
  21.7 0.6 collective-permute-start.7
  22.3 0.0 collective-permute-done.x0
  22.3 5.9 %collective-permute-start.2 = (bf16[8,128,256]{2,1,0:T(8,128)(2,1)S(1)}, bf16[8,128,256]{2,1,0:T(8,128)(2,1)S(1)}, u32[]{:S(2)}, u32[]{:S(2)}) collective-permute-start(bf16[8,128,256]{2,1,0:T(8,128)(2,1)S(1)} %collective-permute-done.x0), channel_id=1, source_target_pairs={{0,2},{1,3},{2,0},{3,1},{4,6},{5,7},{6,4},{7,5},{8,10},{9,11},{10,... | collective-permute-start | bytes 1572872 | tf_op jit(solution)/shard_map/ppermute | solution.py:189
  28.2 0.4 collective-permute-start.1
  28.6 11.8 %collective-permute-done.2.x2 = bf16[8,128,256]{2,1,0:T(8,128)(2,1)S(1)} collective-permute-done((bf16[8,128,256]{2,1,0:T(8,128)(2,1)S(1)}, bf16[8,128,256]{2,1,0:T(8,128)(2,1)S(1)}, u32[]{:S(2)}, u32[]{:S(2)}) %collective-permute-start.2) | collective-permute-done | bytes 524320 | tf_op jit(solution)/shard_map/ppermute | solution.py:189
  40.4 0.7 collective-permute-start.3
  41.1 1.9 %collective-permute-start.4 = (f32[8,256]{1,0:T(8,128)S(1)}, f32[8,256]{1,0:T(8,128)S(1)}, u32[]{:S(2)}, u32[]{:S(2)}) collective-permute-start(f32[8,256]{1,0:T(8,128)S(1)} %add_rsqrt_fusion.inv_ref), channel_id=1, source_target_pairs={{0,8},{1,5},{4,12},{5,9},{6,2},{8,16},{9,13},{10,6},{11,3},{12,20}... | collective-permute-start | bytes 24584 | tf_op jit(solution)/shard_map/ppermute | solution.py:198
  43.0 4.0 %collective-permute-done.4 = f32[8,256]{1,0:T(8,128)S(1)} collective-permute-done((f32[8,256]{1,0:T(8,128)S(1)}, f32[8,256]{1,0:T(8,128)S(1)}, u32[]{:S(2)}, u32[]{:S(2)}) %collective-permute-start.4) | collective-permute-done | bytes 8224 | tf_op jit(solution)/shard_map/ppermute | solution.py:198
  47.0 9.3 %all-gather.1 = f32[32,256]{1,0:T(8,128)S(1)} all-gather(f32[8,256]{1,0:T(8,128)S(1)} %collective-permute-done.4), channel_id=3, replica_groups=mesh['wide'=64,'narrow'=4] {'narrow'}, dimensions={0}, use_global_device_ids=true | all-gather | bytes 40960 | tf_op jit(solution)/shard_map/all_gather | solution.py:243
  56.2 0.0 collective-permute-done.7
  56.2 0.3 convert_add_fusion
  56.6 1.6 %forward.1 = (bf16[2,8,32,256]{3,2,1,0:T(8,128)(2,1)S(1)}, bf16[2,8,32,256]{3,2,1,0:T(8,128)(2,1)S(1)}) custom-call(s32[1]{0:T(128)} %bitcast.place_ref, s32[1]{0:T(128)S(6)} %copy.12.count_ref, s32[64]{0:T(128)S(1)} %broadcast_subtract_fusion.rows_ref, s32[64]{0:T(128)S(1)} %fusion.7.slots_ref, bf16[64,256,256]{2,1,0:T(8,128)(2,1)S(1)} %bitcast.27, ...), custom_call_target="tpu_custom_call" | custom-call | tf_op jit(solution)/shard_map/forward/pallas_call | solution.py:244
  58.2 0.8 collective-permute-start.5
  58.9 0.1 fusion.2
  59.0 3.7 %collective-permute-start.8 = (bf16[8,128,256]{2,1,0:T(8,128)(2,1)S(1)}, bf16[8,128,256]{2,1,0:T(8,128)(2,1)S(1)}, u32[]{:S(2)}, u32[]{:S(2)}) collective-permute-start(bf16[8,128,256]{2,1,0:T(8,128)(2,1)S(1)} %fusion.2), channel_id=1, source_target_pairs={{0,2},{1,3},{2,0},{3,1},{4,6},{5,7},{6,4},{7,5},{8,10},{9,11},{10,... | collective-permute-start | bytes 1572872 | tf_op jit(solution)/shard_map/ppermute | solution.py:189
  62.7 0.0 collective-permute-done.5
  62.7 0.1 convert_add_fusion.2
  62.8 1.1 collective-permute-start.6
  63.9 13.9 %collective-permute-done.6.other_ref = bf16[8,32,256]{2,1,0:T(8,128)(2,1)S(1)} collective-permute-done((bf16[8,32,256]{2,1,0:T(8,128)(2,1)S(1)}, bf16[8,32,256]{2,1,0:T(8,128)(2,1)S(1)}, u32[]{:S(2)}, u32[]{:S(2)}) %collective-permute-start.6) | collective-permute-done | bytes 131104 | tf_op jit(solution)/shard_map/ppermute | solution.py:189
  77.8 0.2 aggregate.1
  78.1 1.1 broadcast_in_dim.4
  79.2 8.7 %all-to-all-start = ((bf16[64,32,256]{2,1,0:T(8,128)(2,1)}), bf16[64,32,256]{2,1,0:T(8,128)(2,1)S(1)}, u32[]{:S(2)}, u32[]{:S(2)}) async-start(bf16[64,32,256]{2,1,0:T(8,128)(2,1)} %broadcast_in_dim.4), calls=%async_computation | async-start | bytes 2097152 | tf_op jit(solution)/shard_map/all_to_all | solution.py:264
  87.9 1.4 fusion.1
  89.3 4.6 %collective-permute-start.9 = (bf16[8,128,256]{2,1,0:T(8,128)(2,1)S(1)}, bf16[8,128,256]{2,1,0:T(8,128)(2,1)S(1)}, u32[]{:S(2)}, u32[]{:S(2)}) collective-permute-start(bf16[8,128,256]{2,1,0:T(8,128)(2,1)S(1)} %fusion.1), channel_id=1, source_target_pairs={{2,6},{3,11},{5,1},{6,10},{7,15},{8,0},{9,5},{10,14},{11,19},{12,4... | collective-permute-start | bytes 1572872 | tf_op jit(solution)/shard_map/ppermute | solution.py:198
  93.9 29.6 %collective-permute-done.9 = bf16[8,128,256]{2,1,0:T(8,128)(2,1)S(1)} collective-permute-done((bf16[8,128,256]{2,1,0:T(8,128)(2,1)S(1)}, bf16[8,128,256]{2,1,0:T(8,128)(2,1)S(1)}, u32[]{:S(2)}, u32[]{:S(2)}) %collective-permute-start.9) | collective-permute-done | bytes 524320 | tf_op jit(solution)/shard_map/ppermute | solution.py:198
  123.5 0.8 copy-done.5
  124.3 1.2 convert_add_fusion.1
  125.6 4.6 %collective-permute-start.10 = (bf16[2,2,128,256]{3,2,1,0:T(8,128)(2,1)S(1)}, bf16[2,2,128,256]{3,2,1,0:T(8,128)(2,1)S(1)}, u32[]{:S(2)}, u32[]{:S(2)}) collective-permute-start(bf16[2,2,128,256]{3,2,1,0:T(8,128)(2,1)S(1)} %pad_maximum_fusion), channel_id=1, source_target_pairs={{0,1},{1,0},{2,3},{3,2},{4,5},{5,4},{6,7},{7,6},{8,9},{9,8},{10,11... | collective-permute-start | bytes 786440 | tf_op jit(solution)/shard_map/ppermute | solution.py:189
  130.2 1.2 collective-permute-done.10
  131.4 0.1 fusion.6
  131.5 0.1 collective-permute-start.11
  131.6 9.4 %all-gather.2 = bf16[32,32,256]{2,1,0:T(8,128)(2,1)S(1)} all-gather(bf16[8,32,256]{2,1,0:T(8,128)(2,1)S(1)} %get-tuple-element.13), channel_id=4, replica_groups=mesh['wide'=64,'narrow'=4] {'narrow'}, dimensions={0}, use_global_device_ids=true | all-gather | bytes 655360 | tf_op jit(solution)/shard_map/all_gather | solution.py:268
  141.0 2.3 %out.1 = bf16[8,256,256]{2,1,0:T(8,128)(2,1)} custom-call(bf16[4,8,32,256]{3,2,1,0:T(8,128)(2,1)S(1)} %bitcast.30, bf16[128,256]{1,0:T(8,128)(2,1)S(1)} %copy-done.3), custom_call_target="tpu_custom_call" | custom-call | tf_op jit(solution)/shard_map/out/pallas_call | solution.py:269
  143.3 0.1 grad.1
  143.4 7.3 %all_gather.30 = bf16[8,256,128]{2,1,0:T(8,128)(2,1)S(1)} all-gather(bf16[2,256,128]{2,1,0:T(8,128)(2,1)S(1)} %grad.1), channel_id=1, replica_groups=mesh['wide'=64,'narrow'=4] {'narrow'}, dimensions={0}, use_global_device_ids=true | all-gather | bytes 655360 | tf_op jit(solution)/shard_map/all_gather | solution.py:284
  150.7 0.2 convert_reduce_fusion
  150.9 5.4 %all_gather.31 = f32[128,256]{1,0:T(8,128)S(1)} all-gather(f32[32,256]{1,0:T(8,128)S(1)} %convert_reduce_fusion), channel_id=1, replica_groups=mesh['wide'=64,'narrow'=4] {'narrow'}, dimensions={0}, use_global_device_ids=true | all-gather | bytes 163840 | tf_op jit(solution)/shard_map/all_gather | solution.py:266
  156.3 0.8 copy.13
  157.1 0.7 copy.14
  (28 shorter events, 0.2 us)
Async XLA Ops:
  0.6 1.0 copy-start.2
  1.9 20.5 %collective-permute-start = (bf16[8,128,256]{2,1,0:T(8,128)(2,1)S(1)}, bf16[8,128,256]{2,1,0:T(8,128)(2,1)S(1)}, u32[]{:S(2)}, u32[]{:S(2)}) collective-permute-start(bf16[8,128,256]{2,1,0:T(8,128)(2,1)S(1)} %turn.1.own_ref.feats_ref), channel_id=1, source_target_pairs={{0,8},{1,5},{4,12},{5,9},{6,2},{8,16},{9,13},{10,6},{11,3},{12,20}... | collective-permute-start | bytes 1572872 | tf_op jit(solution)/shard_map/ppermute | solution.py:198
  9.1 3.4 %copy-start = (bf16[64,256,256]{2,1,0:T(8,128)(2,1)S(1)}, bf16[64,256,256]{2,1,0:T(8,128)(2,1)}, u32[]{:S(2)}) copy-start(bf16[64,256,256]{2,1,0:T(8,128)(2,1)} %tiles_ref.5) | copy-start | bytes 25165828
  12.5 7.3 %copy-start.6 = (s32[64]{0:T(128)S(1)}, s32[64]{0:T(128)}, u32[]{:S(2)}) copy-start(s32[64]{0:T(128)} %param.10) | copy-start | bytes 772
  12.5 7.3 %copy-start.1 = (bf16[2048,256]{1,0:T(8,128)(2,1)S(1)}, bf16[2048,256]{1,0:T(8,128)(2,1)}, u32[]{:S(2)}) copy-start(bf16[2048,256]{1,0:T(8,128)(2,1)} %param.13) | copy-start | bytes 3145732
  12.5 7.3 %copy-start.3 = (bf16[128,256]{1,0:T(8,128)(2,1)S(1)}, bf16[128,256]{1,0:T(8,128)(2,1)}, u32[]{:S(2)}) copy-start(bf16[128,256]{1,0:T(8,128)(2,1)} %weight_ref.3) | copy-start | bytes 196612
  12.5 44.1 %slice-start = ((s8[8388608]{0:T(1024)(128)(4,1)}), s8[4194304]{0:T(1024)(128)(4,1)S(1)}, s32[]{:S(2)}) async-start(s8[8388608]{0:T(1024)(128)(4,1)} %bitcast.26), calls=%async_computation.1 | async-start | bytes 8388608
  19.8 36.7 %slice-start.1 = ((s8[8388608]{0:T(1024)(128)(4,1)}), s8[4194304]{0:T(1024)(128)(4,1)S(1)}, s32[]{:S(2)}) async-start(s8[8388608]{0:T(1024)(128)(4,1)} %bitcast.26), calls=%async_computation.2 | async-start | bytes 8388608
  21.7 34.5 %collective-permute-start.7 = (bf16[2,8,128,256]{3,2,1,0:T(8,128)(2,1)S(1)}, bf16[2,8,128,256]{3,2,1,0:T(8,128)(2,1)S(1)}, u32[]{:S(2)}, u32[]{:S(2)}) collective-permute-start(bf16[2,8,128,256]{3,2,1,0:T(8,128)(2,1)S(1)} %get-tuple-element.16), channel_id=1, source_target_pairs={{0,1},{1,0},{2,3},{3,2},{4,5},{5,4},{6,7},{7,6},{8,9},{9,8},{10,11... | collective-permute-start | bytes 3145736 | tf_op jit(solution)/shard_map/ppermute | solution.py:189
  22.3 18.1 %collective-permute-start.2 = (bf16[8,128,256]{2,1,0:T(8,128)(2,1)S(1)}, bf16[8,128,256]{2,1,0:T(8,128)(2,1)S(1)}, u32[]{:S(2)}, u32[]{:S(2)}) collective-permute-start(bf16[8,128,256]{2,1,0:T(8,128)(2,1)S(1)} %collective-permute-done.x0), channel_id=1, source_target_pairs={{0,2},{1,3},{2,0},{3,1},{4,6},{5,7},{6,4},{7,5},{8,10},{9,11},{10,... | collective-permute-start | bytes 1572872 | tf_op jit(solution)/shard_map/ppermute | solution.py:189
  28.2 28.3 %collective-permute-start.1 = (bf16[8,128,256]{2,1,0:T(8,128)(2,1)S(1)}, bf16[8,128,256]{2,1,0:T(8,128)(2,1)S(1)}, u32[]{:S(2)}, u32[]{:S(2)}) collective-permute-start(bf16[8,128,256]{2,1,0:T(8,128)(2,1)S(1)} %collective-permute-done.x0), channel_id=1, source_target_pairs={{0,1},{1,0},{2,3},{3,2},{4,5},{5,4},{6,7},{7,6},{8,9},{9,8},{10,11... | collective-permute-start | bytes 1572872 | tf_op jit(solution)/shard_map/ppermute | solution.py:189
  40.4 16.1 %collective-permute-start.3 = (bf16[8,128,256]{2,1,0:T(8,128)(2,1)S(1)}, bf16[8,128,256]{2,1,0:T(8,128)(2,1)S(1)}, u32[]{:S(2)}, u32[]{:S(2)}) collective-permute-start(bf16[8,128,256]{2,1,0:T(8,128)(2,1)S(1)} %collective-permute-done.2.x2), channel_id=1, source_target_pairs={{0,1},{1,0},{2,3},{3,2},{4,5},{5,4},{6,7},{7,6},{8,9},{9,8},{10,11... | collective-permute-start | bytes 1572872 | tf_op jit(solution)/shard_map/ppermute | solution.py:189
  41.1 5.9 %collective-permute-start.4 = (f32[8,256]{1,0:T(8,128)S(1)}, f32[8,256]{1,0:T(8,128)S(1)}, u32[]{:S(2)}, u32[]{:S(2)}) collective-permute-start(f32[8,256]{1,0:T(8,128)S(1)} %add_rsqrt_fusion.inv_ref), channel_id=1, source_target_pairs={{0,8},{1,5},{4,12},{5,9},{6,2},{8,16},{9,13},{10,6},{11,3},{12,20}... | collective-permute-start | bytes 24584 | tf_op jit(solution)/shard_map/ppermute | solution.py:198
  56.5 2.4 %copy-start.4 = (f32[2,8,128,256]{3,2,1,0:T(8,128)}, f32[2,8,128,256]{3,2,1,0:T(8,128)S(1)}, u32[]{:S(2)}) copy-start(f32[2,8,128,256]{3,2,1,0:T(8,128)S(1)} %convert_add_fusion) | copy-start | bytes 6291460
  58.2 4.6 %collective-permute-start.5 = (bf16[2,8,32,256]{3,2,1,0:T(8,128)(2,1)S(1)}, bf16[2,8,32,256]{3,2,1,0:T(8,128)(2,1)S(1)}, u32[]{:S(2)}, u32[]{:S(2)}) collective-permute-start(bf16[2,8,32,256]{3,2,1,0:T(8,128)(2,1)S(1)} %get-tuple-element.12), channel_id=1, source_target_pairs={{0,1},{1,0},{2,3},{3,2},{4,5},{5,4},{6,7},{7,6},{8,9},{9,8},{10,11... | collective-permute-start | bytes 786440 | tf_op jit(solution)/shard_map/ppermute | solution.py:189
  59.0 28.9 %collective-permute-start.8 = (bf16[8,128,256]{2,1,0:T(8,128)(2,1)S(1)}, bf16[8,128,256]{2,1,0:T(8,128)(2,1)S(1)}, u32[]{:S(2)}, u32[]{:S(2)}) collective-permute-start(bf16[8,128,256]{2,1,0:T(8,128)(2,1)S(1)} %fusion.2), channel_id=1, source_target_pairs={{0,2},{1,3},{2,0},{3,1},{4,6},{5,7},{6,4},{7,5},{8,10},{9,11},{10,... | collective-permute-start | bytes 1572872 | tf_op jit(solution)/shard_map/ppermute | solution.py:189
  62.8 15.0 %collective-permute-start.6 = (bf16[8,32,256]{2,1,0:T(8,128)(2,1)S(1)}, bf16[8,32,256]{2,1,0:T(8,128)(2,1)S(1)}, u32[]{:S(2)}, u32[]{:S(2)}) collective-permute-start(bf16[8,32,256]{2,1,0:T(8,128)(2,1)S(1)} %fusion.5), channel_id=1, source_target_pairs={{0,2},{1,3},{2,0},{3,1},{4,6},{5,7},{6,4},{7,5},{8,10},{9,11},{10,... | collective-permute-start | bytes 393224 | tf_op jit(solution)/shard_map/ppermute | solution.py:189
  79.2 71.5 %all-to-all-start = ((bf16[64,32,256]{2,1,0:T(8,128)(2,1)}), bf16[64,32,256]{2,1,0:T(8,128)(2,1)S(1)}, u32[]{:S(2)}, u32[]{:S(2)}) async-start(bf16[64,32,256]{2,1,0:T(8,128)(2,1)} %broadcast_in_dim.4), calls=%async_computation | async-start | bytes 2097152 | tf_op jit(solution)/shard_map/all_to_all | solution.py:264
  89.3 34.2 %collective-permute-start.9 = (bf16[8,128,256]{2,1,0:T(8,128)(2,1)S(1)}, bf16[8,128,256]{2,1,0:T(8,128)(2,1)S(1)}, u32[]{:S(2)}, u32[]{:S(2)}) collective-permute-start(bf16[8,128,256]{2,1,0:T(8,128)(2,1)S(1)} %fusion.1), channel_id=1, source_target_pairs={{2,6},{3,11},{5,1},{6,10},{7,15},{8,0},{9,5},{10,14},{11,19},{12,4... | collective-permute-start | bytes 1572872 | tf_op jit(solution)/shard_map/ppermute | solution.py:198
  123.5 0.8 copy-start.5
  125.6 5.8 %collective-permute-start.10 = (bf16[2,2,128,256]{3,2,1,0:T(8,128)(2,1)S(1)}, bf16[2,2,128,256]{3,2,1,0:T(8,128)(2,1)S(1)}, u32[]{:S(2)}, u32[]{:S(2)}) collective-permute-start(bf16[2,2,128,256]{3,2,1,0:T(8,128)(2,1)S(1)} %pad_maximum_fusion), channel_id=1, source_target_pairs={{0,1},{1,0},{2,3},{3,2},{4,5},{5,4},{6,7},{7,6},{8,9},{9,8},{10,11... | collective-permute-start | bytes 786440 | tf_op jit(solution)/shard_map/ppermute | solution.py:189
  131.5 11.8 %collective-permute-start.11 = (bf16[2,128,256]{2,1,0:T(8,128)(2,1)S(1)}, bf16[2,128,256]{2,1,0:T(8,128)(2,1)S(1)}, u32[]{:S(2)}, u32[]{:S(2)}) collective-permute-start(bf16[2,128,256]{2,1,0:T(8,128)(2,1)S(1)} %get-tuple-element.19), channel_id=1, source_target_pairs={{0,2},{1,3},{2,0},{3,1},{4,6},{5,7},{6,4},{7,5},{8,10},{9,11},{10,... | collective-permute-start | bytes 393224 | tf_op jit(solution)/shard_map/ppermute | solution.py:189

commit v2 on v1

v2 whole, which is shorter than its diff:
```python
import jax
import jax.numpy as jnp
from jax import lax
from jax.experimental import pallas as pl
from jax.experimental.pallas import tpu as pltpu
from jax.sharding import Mesh, PartitionSpec as P

WIDE = ("far", "near")
BLOCK = 256
REACH = 2
STEP = 8
COST = {
    "degree": 10, "scale": 1, "backward": 10, "pass": 1, "forward": 10, "whole": 1,
    "aggregate": 10, "gather": 1, "split": 1, "pack": 1, "grad": 5, "finish": 1, "after": 0,
}
OFFSETS = (-2, -1, 1, 2)
f32 = jnp.float32
bf16 = jnp.bfloat16
VMEM = pl.BlockSpec(memory_space=pltpu.VMEM)
HBM = pl.BlockSpec(memory_space=pltpu.HBM)
SMEM = pl.BlockSpec(memory_space=pltpu.SMEM)

NT = (((1,), (1,)), ((), ()))
TN = (((0,), (0,)), ((), ()))


def shape(dims, dtype):
    return jax.ShapeDtypeStruct(dims, dtype)


def call(kernel, ins, outs, scratch=(), name=None, mib=6):
    return pl.pallas_call(
        kernel,
        in_specs=ins,
        out_specs=[VMEM] * len(outs),
        out_shape=outs,
        scratch_shapes=list(scratch),
        compiler_params=pltpu.CompilerParams(vmem_limit_bytes=mib * 2**20),
        cost_estimate=pl.CostEstimate(
            flops=COST[name] * 10**9, bytes_accessed=COST[name] * 10**6, transcendentals=0
        ),
        name=name,
    )


def each_step(count, step_fn):
    def body(step, carry):
        step_fn(step * STEP)
        return carry

    lax.fori_loop(0, (count + STEP - 1) // STEP, body, 0)


def after(x, *others, first=False):
    def kernel(*refs):
        refs[-1][...] = refs[0][0] if first else refs[0][...]

    (out,) = call(
        kernel, [VMEM] * (1 + len(others)), [shape(x.shape[first:], x.dtype)], name="after"
    )(x, *others)
    return out


def scale_kernel(degrees_ref, feats_ref, inv_ref, out_ref):
    degree = 1.0 + degrees_ref[0]
    for part in range(1, degrees_ref.shape[0]):
        degree = degree + degrees_ref[part]
    inv_ref[...] = lax.rsqrt(degree)
    for block in range(out_ref.shape[0]):
        turned = feats_ref[block].T.astype(f32)
        out_ref[block] = (turned * inv_ref[block : block + 1]).astype(bf16)


def degree_kernel(count_ref, rows_ref, tiles_ref, out_ref, total):
    blocks = out_ref.shape[0]
    count = count_ref[0]
    ones = jnp.ones((8, BLOCK), bf16)

    def prepare():
        total[...] = jnp.zeros_like(total)

    def step_fn(first):
        sums = [
            lax.dot_general(ones, tiles_ref[first + k], NT, preferred_element_type=f32)
            for k in range(STEP)
        ]
        for k in range(STEP):
            row = jnp.where(first + k < count, rows_ref[first + k], blocks)
            total[row] += sums[k]

    prepare()
    each_step(count, step_fn)
    for block in range(blocks):
        out_ref[block : block + 1] = total[block, 0:1]


def backward_kernel(
    count_ref, rows_ref, slots_ref, tiles_ref, weight_ref, cot_ref, inv_ref,
    back_ref, own_ref, keep0_ref, keep2_ref, send1_ref, send3a_ref, send3b_ref, total,
):
    blocks = cot_ref.shape[0]
    count = count_ref[0]

    def prepare():
        for block in range(blocks):
            rows = lax.dot_general(weight_ref[...], cot_ref[block], NT, preferred_element_type=f32)
            back_ref[block] = (rows * inv_ref[block : block + 1]).astype(bf16)
        total[...] = jnp.zeros_like(total)

    def step_fn(first):
        products = [
            jnp.dot(back_ref[rows_ref[first + k]], tiles_ref[first + k], preferred_element_type=f32)
            for k in range(STEP)
        ]
        for k in range(STEP):
            slot = jnp.where(first + k < count, slots_ref[first + k], 5 * blocks)
            total[slot] += products[k]

    prepare()
    each_step(count, step_fn)
    half = blocks // 2
    for part, ref in enumerate((own_ref, keep0_ref, send1_ref, keep2_ref)):
        for block in range(blocks):
            ref[block] = total[part * blocks + block].astype(bf16)
    for block in range(half):
        send3a_ref[block] = total[4 * blocks + block].astype(bf16)
        send3b_ref[block] = total[4 * blocks + half + block].astype(bf16)


def pass_kernel(keep_ref, a_ref, b_ref, out_ref):
    half = a_ref.shape[0]
    for block in range(half):
        got = a_ref[block].astype(f32)
        out_ref[block] = (keep_ref[block].astype(f32) + got).astype(bf16)
        got = b_ref[block].astype(f32)
        out_ref[half + block] = (keep_ref[half + block].astype(f32) + got).astype(bf16)


def forward_kernel(
    place_ref, count_ref, rows_ref, slots_ref, tiles_ref, own_ref, x0, x1, x2, x3, ready_ref,
    keep_ref, send_ref, window, total,
):
    blocks = own_ref.shape[0]
    quarter = own_ref.shape[1] // 4
    count = count_ref[0]
    me = place_ref[0]

    def prepare():
        for part, ref in enumerate((own_ref, x0, x1, x2, x3)):
            for block in range(blocks):
                window[part * blocks + block] = ref[block]
        total[...] = jnp.zeros_like(total)

    def step_fn(first):
        products = [
            lax.dot_general(
                window[slots_ref[first + k]], tiles_ref[first + k], NT, preferred_element_type=f32
            )
            for k in range(STEP)
        ]
        for k in range(STEP):
            row = jnp.where(first + k < count, rows_ref[first + k], blocks)
            total[row] += products[k]

    prepare()
    each_step(count, step_fn)
    for ref, at, part in ((keep_ref, 0, 0), (send_ref, 0, 1), (keep_ref, 1, 2), (send_ref, 1, 3)):
        start = pl.multiple_of((me ^ part) * quarter, quarter)
        for block in range(blocks):
            ref[at, block] = total[block, pl.ds(start, quarter)].astype(bf16)


def whole_kernel(keep_ref, got_ref, other_ref, ready_ref, out_ref):
    for block in range(out_ref.shape[0]):
        whole = keep_ref[block].astype(f32) + got_ref[block].astype(f32)
        out_ref[block] = (whole + other_ref[block].astype(f32)).astype(bf16)


def aggregate_kernel(
    place_ref, mine_ref, got_ref, other_ref, inv_ref, scaled_ref, cot_ref, agg_ref, terms_ref
):
    blocks = other_ref.shape[0]
    quarter = other_ref.shape[1]
    start = pl.multiple_of(place_ref[0] * quarter, quarter)
    term = jnp.zeros(terms_ref.shape[1:], f32)
    for block in range(blocks):
        inv = inv_ref[block : block + 1]
        own = scaled_ref[block, pl.ds(start, quarter)]
        summed = mine_ref[0, block].astype(f32) + got_ref[0, block].astype(f32)
        summed = summed + other_ref[block].astype(f32)
        agg = (inv * (summed + own.astype(f32))).astype(bf16)
        agg_ref[block] = agg
        term = term + jnp.dot(agg, cot_ref[block], preferred_element_type=f32)
    term = term.astype(bf16)
    for part in range(terms_ref.shape[0]):
        terms_ref[part] = term


def gather_kernel(terms_ref, out_ref):
    total = terms_ref[0].astype(f32)
    for part in range(1, terms_ref.shape[0]):
        total = total + terms_ref[part].astype(f32)
    for part in range(out_ref.shape[0]):
        out_ref[part] = total.astype(bf16)


def split_kernel(place_ref, own_ref, far_ref, ready_ref, also_ref, keep_ref, send_ref):
    for ref, at, part in ((keep_ref, 0, 0), (send_ref, 0, 1), (keep_ref, 1, 2), (send_ref, 1, 3)):
        first = (place_ref[0] ^ part) * 2
        for k in range(2):
            total = own_ref[first + k].astype(f32) + far_ref[first + k].astype(f32)
            ref[at, k] = total.astype(bf16)


def grad_kernel(place_ref, keep_ref, got_ref, other_ref, back_ref, inv_ref, out_ref):
    first = place_ref[0] * 2
    for k in range(2):
        inv = inv_ref[pl.ds(first + k, 1)]
        summed = keep_ref[0, k].astype(f32) + got_ref[0, k].astype(f32)
        summed = summed + other_ref[k].astype(f32)
        out_ref[k] = (inv * (summed + back_ref[first + k].astype(f32))).astype(bf16)


def pack_kernel(terms_ref, grad_ref, out_ref):
    quarter = terms_ref.shape[1]
    width = grad_ref.shape[1]
    total = terms_ref[0].astype(f32)
    for part in range(1, terms_ref.shape[0]):
        total = total + terms_ref[part].astype(f32)
    high = total.astype(bf16)
    out_ref[:quarter] = high
    out_ref[quarter : 2 * quarter] = (total - high.astype(f32)).astype(bf16)
    for k in range(2):
        at = 2 * quarter + k * width
        out_ref[at : at + width] = grad_ref[k]


def finish_kernel(
    place_ref, packed_ref, agg0, agg2, agg13, weight_ref, out_ref, grad_ref, weight_grad_ref
):
    parts = packed_ref.shape[0]
    width = weight_ref.shape[0]
    quarter = width // parts
    blocks = out_ref.shape[0] // BLOCK
    for part in range(parts):
        high = packed_ref[part, :quarter].astype(f32)
        low = packed_ref[part, quarter : 2 * quarter].astype(f32)
        weight_grad_ref[part * quarter : (part + 1) * quarter] = high + low
    for block in range(blocks):
        total = None
        for part, agg in enumerate((agg0, agg13.at[0], agg2, agg13.at[1])):
            start = pl.multiple_of((place_ref[0] ^ part) * quarter, quarter)
            product = lax.dot_general(
                agg[block], weight_ref[pl.ds(start, quarter)], TN, preferred_element_type=f32
            )
            total = product if total is None else total + product
        out_ref[block * BLOCK : (block + 1) * BLOCK] = total.astype(bf16)
        part, k = divmod(block, blocks // parts)
        at = 2 * quarter + k * width
        grad_ref[block * BLOCK : (block + 1) * BLOCK] = packed_ref[part, at : at + width].T


def per_device(feats, tiles, tile_rows, tile_cols, tile_count, weight, cotangent):
    nodes, width = feats.shape
    hidden = cotangent.shape[1]
    blocks = nodes // BLOCK
    quarter = width // 4
    wides = lax.axis_size(WIDE)
    nears = lax.axis_size("near")
    fars = lax.axis_size("far")
    narrows = lax.axis_size("narrow")
    wide = lax.axis_index(WIDE)
    me = lax.axis_index("narrow").astype(jnp.int32)
    place = me.reshape(1)

    def swap(x, by):
        return lax.ppermute(x, "narrow", [(i, i ^ by) for i in range(narrows)])

    def fetch(x, sign, turned=0):
        pairs = [
            (w * narrows + n, (w + sign * OFFSETS[n ^ turned]) * narrows + n)
            for w in range(wides)
            for n in range(narrows)
            if 0 <= w + sign * OFFSETS[n ^ turned] < wides
        ]
        return lax.ppermute(x, WIDE + ("narrow",), pairs)

    rows = tile_rows - wide * blocks
    offset = tile_cols // blocks - wide
    owner = jnp.where(offset < 0, offset + 2, offset + 1)
    part = jnp.where(offset == 0, 0, 1 + (owner ^ me))
    slots = part * blocks + tile_cols % blocks

    (degree_part,) = call(
        degree_kernel,
        [SMEM, SMEM, VMEM],
        [shape((blocks, BLOCK), f32)],
        [pltpu.VMEM((blocks + 1, 8, BLOCK), f32)],
        name="degree",
        mib=4,
    )(tile_count, rows, tiles)
    block_shape = (blocks, width, BLOCK)
    inv, scaled = call(
        scale_kernel,
        [VMEM] * 2,
        [shape((blocks, BLOCK), f32), shape(block_shape, bf16)],
        name="scale",
    )(lax.all_gather(degree_part, "narrow"), feats.reshape(blocks, BLOCK, width))
    x0 = fetch(scaled, -1)
    x2 = fetch(scaled, -1, 2)

    cot = cotangent.reshape(blocks, BLOCK, hidden)
    half_shape = (blocks // 2, width, BLOCK)
    back, q_own, q_keep0, q_keep2, q_send1, q_send3a, q_send3b = call(
        backward_kernel,
        [SMEM] * 3 + [VMEM] * 4,
        [shape(block_shape, bf16)] * 5 + [shape(half_shape, bf16)] * 2,
        [pltpu.VMEM((5 * blocks + 1, width, BLOCK), f32)],
        name="backward",
        mib=12,
    )(tile_count, rows, slots, tiles, weight, cot, inv)
    (q_pass,) = call(pass_kernel, [VMEM] * 3, [shape(block_shape, bf16)], name="pass")(
        q_keep2, swap(q_send3a, 1), swap(q_send3b, 1)
    )
    q_got = swap(q_send1, 1)
    q_other = swap(q_pass, 2)

    x1 = swap(after(x0, q_pass), 1)
    x3 = swap(after(x2, q_pass), 1)
    p_keep, p_send = call(
        forward_kernel,
        [SMEM] * 4 + [VMEM] * 6 + [HBM],
        [shape((2, blocks, quarter, BLOCK), bf16)] * 2,
        [
            pltpu.VMEM((5 * blocks, width, BLOCK), bf16),
            pltpu.VMEM((blocks + 1, width, BLOCK), f32),
        ],
        name="forward",
        mib=12,
    )(place, tile_count, rows, slots, tiles, scaled, x0, x1, x2, x3, q_other)
    p_got = swap(p_send, 1)
    p_pass = (p_keep[1].astype(f32) + p_got[1].astype(f32)).astype(bf16)
    p_other = swap(p_pass, 2)
    (q_whole,) = call(whole_kernel, [VMEM] * 3 + [HBM], [shape(block_shape, bf16)], name="whole")(
        q_keep0, q_got, q_other, p_pass
    )
    q_far = fetch(q_whole, 1)
    agg, terms = call(
        aggregate_kernel,
        [SMEM] + [VMEM] * 6,
        [
            shape((blocks, quarter, BLOCK), bf16),
            shape((fars, quarter, hidden), bf16),
        ],
        name="aggregate",
    )(place, p_keep, p_got, p_other, inv, scaled, cot)
    terms = lax.all_to_all(terms, "far", 0, 0)
    agg2 = swap(agg, 2)
    agg13 = swap(jnp.stack([agg, agg2]), 1)
    (terms,) = call(
        gather_kernel, [VMEM], [shape((nears, quarter, hidden), bf16)], name="gather"
    )(terms)

    z_keep, z_send = call(
        split_kernel,
        [SMEM] + [VMEM] * 2 + [HBM] * 2,
        [shape((2, 2, width, BLOCK), bf16)] * 2,
        name="split",
    )(place, q_own, q_far, terms, agg2)
    z_got = swap(z_send, 1)
    z_pass = (z_keep[1].astype(f32) + z_got[1].astype(f32)).astype(bf16)
    z_other = swap(z_pass, 2)
    terms = lax.all_to_all(after(terms, z_pass), "near", 0, 0)
    (grad,) = call(
        grad_kernel, [SMEM] + [VMEM] * 5, [shape((2, width, BLOCK), bf16)], name="grad"
    )(place, z_keep, z_got, z_other, back, inv)
    (packed,) = call(
        pack_kernel,
        [VMEM] * 2,
        [shape((2 * quarter + 2 * width, BLOCK), bf16)],
        name="pack",
    )(terms, grad)
    packed = lax.all_gather(packed, "narrow")
    out, feats_grad, weight_grad = call(
        finish_kernel,
        [SMEM] + [VMEM] * 5,
        [
            shape((nodes, hidden), bf16),
            shape((nodes, width), bf16),
            shape((width, hidden), f32),
        ],
        name="finish",
    )(place, packed, agg, agg2, agg13, weight)
    return (out, feats_grad, weight_grad)


def solution(mesh):
    mesh = Mesh(mesh.devices.reshape(8, 8, 4), ("far", "near", "narrow"))
    rows = P(WIDE, None)
    slots = P(WIDE + ("narrow",))
    placed = (rows, P(WIDE + ("narrow",), None, None), slots, slots, slots, P(), rows)
    return jax.shard_map(
        per_device,
        mesh=mesh,
        in_specs=placed,
        out_specs=(rows, rows, P()),
        check_vma=False,
    )
```

time: 159 us -> 108 us (0.68)
  the two profiles are of different devices: /device:TPU:35 before, /device:TPU:1 now
where the time goes in v2:
time: 108 us
  waiting for transfers between devices  37.6 us (35%)
  starting transfers between devices  30.8 us (29%)
  blocking collectives  17.6 us (16%)
  Pallas kernels  11.4 us (11%)
  local copies, waits for them, and re-layouts  7.83 us (7%)
  between operations  1.53 us (1%)
    ppermute x12, waiting for transfers between devices, swap(): return lax.ppermute(x, 'narrow', [(i, i ^ by) for i in range(narrows)])  18.8 us
    ppermute x12, starting transfers between devices, swap(): return lax.ppermute(x, 'narrow', [(i, i ^ by) for i in range(narrows)])  11.9 us
    all_to_all x1, starting transfers between devices, per_device(): terms = lax.all_to_all(terms, 'far', 0, 0)  10.1 us
    all_gather x1, blocking collectives, per_device(): lax.all_gather(degree_part, 'narrow')  9.42 us
    all_gather x1, blocking collectives, per_device(): packed = lax.all_gather(packed, 'narrow')  8.16 us
    all_to_all x1, waiting for transfers between devices, per_device(): terms = lax.all_to_all(terms, 'far', 0, 0)  7.94 us
    unnamed x20, local copies, waits for them, and re-layouts  7.83 us
    all_to_all x1, waiting for transfers between devices, per_device(): terms = lax.all_to_all(after(terms, z_pass), 'near', 0, 0)  6.83 us
  transfers between devices with their start and end apart: 17, of which 10 were waited for; matrix products, arithmetic and copies ran while one was open for 0% of the time, Pallas kernels for 4%

profile of v2, /device:TPU:1, one launch (start us, length us, event | category | flops | bytes accessed | tf_op | source)
XLA Modules:
  0.0 107.6 jit_solution(3006034566009827571)
XLA Ops:
  1.3 0.7 broadcast_subtract_fusion.rows_ref
  1.9 3.4 %copy-done = bf16[64,256,256]{2,1,0:T(8,128)(2,1)S(1)} copy-done((bf16[64,256,256]{2,1,0:T(8,128)(2,1)S(1)}, bf16[64,256,256]{2,1,0:T(8,128)(2,1)}, u32[]{:S(2)}) %copy-start) | copy-done | bytes 8388632
  5.3 1.7 %degree.1 = f32[8,256]{1,0:T(8,128)S(1)} custom-call(s32[1]{0:T(128)S(6)} %copy.10.count_ref, s32[64]{0:T(128)S(1)} %broadcast_subtract_fusion.rows_ref, bf16[64,256,256]{2,1,0:T(8,128)(2,1)S(1)} %copy-done), custom_call_target="tpu_custom_call" | custom-call | flops 10000000000 | bytes 10000000 | tf_op jit(solution)/shard_map/degree/pallas_call | solution.py:294
  7.1 9.4 %all-gather = f32[32,256]{1,0:T(8,128)S(1)} all-gather(f32[8,256]{1,0:T(8,128)S(1)} %degree.1), channel_id=2, replica_groups=mesh['far'=8,'near'=8,'narrow'=4] {'narrow'}, dimensions={0}, use_global_device_ids=true | all-gather | bytes 40960 | tf_op jit(solution)/shard_map/all_gather | solution.py:308
  16.5 0.2 scale.1
  16.7 1.3 %collective-permute-start.4 = (bf16[8,128,256]{2,1,0:T(8,128)(2,1)S(1)}, bf16[8,128,256]{2,1,0:T(8,128)(2,1)S(1)}, u32[]{:S(2)}, u32[]{:S(2)}) collective-permute-start(bf16[8,128,256]{2,1,0:T(8,128)(2,1)S(1)} %get-tuple-element.18.own_ref.scaled_ref), channel_id=1, source_target_pairs={{2,10},{3,7},{4,0},{6,14},{7,11},{8,4},{9,1},{10,18},{11,15},{12,8... | collective-permute-start | bytes 1572872 | tf_op jit(solution)/shard_map/ppermute | solution.py:286
  18.0 1.3 %collective-permute-start = (bf16[8,128,256]{2,1,0:T(8,128)(2,1)S(1)}, bf16[8,128,256]{2,1,0:T(8,128)(2,1)S(1)}, u32[]{:S(2)}, u32[]{:S(2)}) collective-permute-start(bf16[8,128,256]{2,1,0:T(8,128)(2,1)S(1)} %get-tuple-element.18.own_ref.scaled_ref), channel_id=1, source_target_pairs={{0,8},{1,5},{4,12},{5,9},{6,2},{8,16},{9,13},{10,6},{11,3},{12,20}... | collective-permute-start | bytes 1572872 | tf_op jit(solution)/shard_map/ppermute | solution.py:286
  19.4 0.0 copy-start.1
  19.4 3.4 %copy-done.1 = bf16[64,256,256]{2,1,0:T(8,128)(2,1)S(1)} copy-done((bf16[64,256,256]{2,1,0:T(8,128)(2,1)S(1)}, bf16[64,256,256]{2,1,0:T(8,128)(2,1)}, u32[]{:S(2)}) %copy-start.1) | copy-done | bytes 8388632
  22.8 2.5 %backward.1 = (bf16[8,128,256]{2,1,0:T(8,128)(2,1)S(1)}, bf16[8,128,256]{2,1,0:T(8,128)(2,1)S(1)}, bf16[8,128,256]{2,1,0:T(8,128)(2,1)S(1)}, bf16[8,128,256]{2,1...) custom-call(s32[1]{0:T(128)S(6)} %copy.10.count_ref, ...), custom_call_target="tpu_custom_call" | custom-call | flops 10000000000 | bytes 10000000 | tf_op jit(solution)/shard_map/backward/pallas_call | solution.py:314
  25.3 0.0 copy-start.5
  25.3 0.0 copy-start.7
  25.3 3.2 %collective-permute-start.1 = (bf16[4,128,256]{2,1,0:T(8,128)(2,1)S(1)}, bf16[4,128,256]{2,1,0:T(8,128)(2,1)S(1)}, u32[]{:S(2)}, u32[]{:S(2)}) collective-permute-start(bf16[4,128,256]{2,1,0:T(8,128)(2,1)S(1)} %get-tuple-element.21), channel_id=1, source_target_pairs={{0,1},{1,0},{2,3},{3,2},{4,5},{5,4},{6,7},{7,6},{8,9},{9,8},{10,11... | collective-permute-start | bytes 786440 | tf_op jit(solution)/shard_map/ppermute | solution.py:277
  28.6 0.1 collective-permute-start.2
  28.7 1.1 collective-permute-done.1.a_ref
  29.7 0.4 collective-permute-done.2.b_ref
  30.1 0.1 pass.1.refs_1_
  30.2 0.1 collective-permute-start.6
  30.3 4.1 %collective-permute-done.refs_0_.x0 = bf16[8,128,256]{2,1,0:T(8,128)(2,1)S(1)} collective-permute-done((bf16[8,128,256]{2,1,0:T(8,128)(2,1)S(1)}, bf16[8,128,256]{2,1,0:T(8,128)(2,1)S(1)}, u32[]{:S(2)}, u32[]{:S(2)}) %collective-permute-start) | collective-permute-done | bytes 524320 | tf_op jit(solution)/shard_map/ppermute | solution.py:286
  34.5 2.7 %collective-permute-start.3 = (bf16[8,128,256]{2,1,0:T(8,128)(2,1)S(1)}, bf16[8,128,256]{2,1,0:T(8,128)(2,1)S(1)}, u32[]{:S(2)}, u32[]{:S(2)}) collective-permute-start(bf16[8,128,256]{2,1,0:T(8,128)(2,1)S(1)} %after.3), channel_id=1, source_target_pairs={{0,1},{1,0},{2,3},{3,2},{4,5},{5,4},{6,7},{7,6},{8,9},{9,8},{10,11... | collective-permute-start | bytes 1572872 | tf_op jit(solution)/shard_map/ppermute | solution.py:277
  37.2 0.1 collective-permute-start.5
  37.3 11.9 %collective-permute-done.6.ready_ref.other_ref = bf16[8,128,256]{2,1,0:T(8,128)(2,1)S(1)} collective-permute-done((bf16[8,128,256]{2,1,0:T(8,128)(2,1)S(1)}, bf16[8,128,256]{2,1,0:T(8,128)(2,1)S(1)}, u32[]{:S(2)}, u32[]{:S(2)}) %collective-permute-start.6) | collective-permute-done | bytes 524320 | tf_op jit(solution)/shard_map/ppermute | solution.py:277
  49.2 0.0 collective-permute-done.3.x1
  49.2 2.3 %forward.1 = (bf16[2,8,32,256]{3,2,1,0:T(8,128)(2,1)S(1)}, bf16[2,8,32,256]{3,2,1,0:T(8,128)(2,1)S(1)}) custom-call(s32[1]{0:T(128)} %bitcast.place_ref, s32[1]{0:T(128)S(6)} %copy.10.count_ref, s32[64]{0:T(128)S(1)} %broadcast_subtract_fusion.rows_ref, s32[64]{0:T(128)S(1)} %fusion.2.slots_ref, bf16[64,256,256]{2,1,0:T(8,128)(2,1)S(1)} %copy-done.1, ...), custom_call_target="tpu_custom_call" | custom-call | flops 10000000000 | bytes 10000000 | tf_op jit(solution)/shard_map/forward/pallas_call | solution.py:330
  51.5 2.0 %collective-permute-start.7 = (bf16[2,8,32,256]{3,2,1,0:T(8,128)(2,1)S(1)}, bf16[2,8,32,256]{3,2,1,0:T(8,128)(2,1)S(1)}, u32[]{:S(2)}, u32[]{:S(2)}) collective-permute-start(bf16[2,8,32,256]{3,2,1,0:T(8,128)(2,1)S(1)} %get-tuple-element.24), channel_id=1, source_target_pairs={{0,1},{1,0},{2,3},{3,2},{4,5},{5,4},{6,7},{7,6},{8,9},{9,8},{10,11... | collective-permute-start | bytes 786440 | tf_op jit(solution)/shard_map/ppermute | solution.py:277
  53.6 0.1 collective-permute-start.9
  53.7 1.1 collective-permute-done.7.got_ref
  54.8 0.1 collective-permute-start.8
  54.9 0.6 collective-permute-done.9.got_ref
  55.5 0.2 whole.1
  55.7 1.3 %collective-permute-start.10 = (bf16[8,128,256]{2,1,0:T(8,128)(2,1)S(1)}, bf16[8,128,256]{2,1,0:T(8,128)(2,1)S(1)}, u32[]{:S(2)}, u32[]{:S(2)}) collective-permute-start(bf16[8,128,256]{2,1,0:T(8,128)(2,1)S(1)} %whole.1), channel_id=1, source_target_pairs={{2,6},{3,11},{5,1},{6,10},{7,15},{8,0},{9,5},{10,14},{11,19},{12,4... | collective-permute-start | bytes 1572872 | tf_op jit(solution)/shard_map/ppermute | solution.py:286
  57.0 2.6 %collective-permute-done.8.other_ref = bf16[8,32,256]{2,1,0:T(8,128)(2,1)S(1)} collective-permute-done((bf16[8,32,256]{2,1,0:T(8,128)(2,1)S(1)}, bf16[8,32,256]{2,1,0:T(8,128)(2,1)S(1)}, u32[]{:S(2)}, u32[]{:S(2)}) %collective-permute-start.8) | collective-permute-done | bytes 131104 | tf_op jit(solution)/shard_map/ppermute | solution.py:277
  59.6 0.9 aggregate.1
  60.5 10.1 %all-to-all-start = ((bf16[8,32,256]{2,1,0:T(8,128)(2,1)}), bf16[8,32,256]{2,1,0:T(8,128)(2,1)S(1)}, u32[]{:S(2)}, u32[]{:S(2)}) async-start(bf16[8,32,256]{2,1,0:T(8,128)(2,1)} %get-tuple-element.25), calls=%async_computation | async-start | bytes 262144 | tf_op jit(solution)/shard_map/all_to_all | solution.py:357
  70.6 7.9 %all-to-all-done.terms_ref = bf16[8,32,256]{2,1,0:T(8,128)(2,1)S(1)} async-done(((bf16[8,32,256]{2,1,0:T(8,128)(2,1)}), bf16[8,32,256]{2,1,0:T(8,128)(2,1)S(1)}, u32[]{:S(2)}, u32[]{:S(2)}) %all-to-all-start) | async-done | bytes 131104 | tf_op jit(solution)/shard_map/all_to_all | solution.py:357
  78.6 0.0 copy-start.6
  78.6 1.0 copy-done.6
  79.7 0.1 split.1
  79.8 2.9 %collective-permute-start.12 = (bf16[2,2,128,256]{3,2,1,0:T(8,128)(2,1)S(1)}, bf16[2,2,128,256]{3,2,1,0:T(8,128)(2,1)S(1)}, u32[]{:S(2)}, u32[]{:S(2)}) collective-permute-start(bf16[2,2,128,256]{3,2,1,0:T(8,128)(2,1)S(1)} %get-tuple-element.31), channel_id=1, source_target_pairs={{0,1},{1,0},{2,3},{3,2},{4,5},{5,4},{6,7},{7,6},{8,9},{9,8},{10,11... | collective-permute-start | bytes 786440 | tf_op jit(solution)/shard_map/ppermute | solution.py:277
  82.7 1.2 %collective-permute-done.12.got_ref = bf16[2,2,128,256]{3,2,1,0:T(8,128)(2,1)S(1)} collective-permute-done((bf16[2,2,128,256]{3,2,1,0:T(8,128)(2,1)S(1)}, bf16[2,2,128,256]{3,2,1,0:T(8,128)(2,1)S(1)}, u32[]{:S(2)}, u32[]{:S(2)}) %collective-permute-start.12) | collective-permute-done | bytes 262176 | tf_op jit(solution)/shard_map/ppermute | solution.py:277
  83.9 0.1 collective-permute-start.13
  84.0 0.5 collective-permute-start.14
  84.5 0.7 after.5
  85.2 4.9 %all-to-all-start.1 = ((bf16[8,32,256]{2,1,0:T(8,128)(2,1)}), bf16[8,32,256]{2,1,0:T(8,128)(2,1)S(1)}, u32[]{:S(2)}, u32[]{:S(2)}) async-start(bf16[8,32,256]{2,1,0:T(8,128)(2,1)} %after.5), calls=%async_computation.1 | async-start | bytes 262144 | tf_op jit(solution)/shard_map/all_to_all | solution.py:373
  90.0 0.1 grad.1.grad_ref
  90.1 6.8 %all-to-all-done.1.terms_ref = bf16[8,32,256]{2,1,0:T(8,128)(2,1)S(1)} async-done(((bf16[8,32,256]{2,1,0:T(8,128)(2,1)}), bf16[8,32,256]{2,1,0:T(8,128)(2,1)S(1)}, u32[]{:S(2)}, u32[]{:S(2)}) %all-to-all-start.1) | async-done | bytes 131104 | tf_op jit(solution)/shard_map/all_to_all | solution.py:373
  97.0 8.2 %all-gather.1 = bf16[1280,256]{1,0:T(8,128)(2,1)S(1)} all-gather(bf16[320,256]{1,0:T(8,128)(2,1)S(1)} %pack.1), channel_id=3, replica_groups=mesh['far'=8,'near'=8,'narrow'=4] {'narrow'}, dimensions={0}, use_global_device_ids=true | all-gather | bytes 819200 | tf_op jit(solution)/shard_map/all_gather | solution.py:383
  105.1 2.4 %finish.1 = (bf16[2048,256]{1,0:T(8,128)(2,1)}, bf16[2048,128]{1,0:T(8,128)(2,1)}, f32[128,256]{1,0:T(8,128)}) custom-call(s32[1]{0:T(128)} %bitcast.place_ref, bf16[4,320,256]{2,1,0:T(8,128)(2,1)S(1)} %bitcast.11, bf16[8,32,256]{2,1,0:T(8,128)(2,1)S(1)} %get-tuple-element.29.agg0, bf16[8,32,256]{2,1,0:T(8,128)(2,1)S(1)} %collective-permute-done.11.also_ref.agg2, ...), custom_call_target="tpu_custom_call" | custom-call | flops 1000000000 | bytes 1000000 | tf_op jit(solution)/shard_map/finish/pallas_call | solution.py:384
  (28 shorter events, 0.3 us)
Async XLA Ops:
  1.9 3.4 %copy-start = (bf16[64,256,256]{2,1,0:T(8,128)(2,1)S(1)}, bf16[64,256,256]{2,1,0:T(8,128)(2,1)}, u32[]{:S(2)}) copy-start(bf16[64,256,256]{2,1,0:T(8,128)(2,1)} %tiles_ref.5) | copy-start | bytes 25165828
  5.3 11.2 %copy-start.3 = (bf16[2048,128]{1,0:T(8,128)(2,1)S(1)}, bf16[2048,128]{1,0:T(8,128)(2,1)}, u32[]{:S(2)}) copy-start(bf16[2048,128]{1,0:T(8,128)(2,1)} %param.7) | copy-start | bytes 1572868
  5.3 14.0 %copy-start.9 = (s32[64]{0:T(128)S(1)}, s32[64]{0:T(128)}, u32[]{:S(2)}) copy-start(s32[64]{0:T(128)} %param.10) | copy-start | bytes 772
  5.3 14.0 %copy-start.2 = (bf16[2048,256]{1,0:T(8,128)(2,1)S(1)}, bf16[2048,256]{1,0:T(8,128)(2,1)}, u32[]{:S(2)}) copy-start(bf16[2048,256]{1,0:T(8,128)(2,1)} %param.13) | copy-start | bytes 3145732
  5.3 14.0 %copy-start.4 = (bf16[128,256]{1,0:T(8,128)(2,1)S(1)}, bf16[128,256]{1,0:T(8,128)(2,1)}, u32[]{:S(2)}) copy-start(bf16[128,256]{1,0:T(8,128)(2,1)} %weight_ref.3) | copy-start | bytes 196612
  16.7 20.5 %collective-permute-start.4 = (bf16[8,128,256]{2,1,0:T(8,128)(2,1)S(1)}, bf16[8,128,256]{2,1,0:T(8,128)(2,1)S(1)}, u32[]{:S(2)}, u32[]{:S(2)}) collective-permute-start(bf16[8,128,256]{2,1,0:T(8,128)(2,1)S(1)} %get-tuple-element.18.own_ref.scaled_ref), channel_id=1, source_target_pairs={{2,10},{3,7},{4,0},{6,14},{7,11},{8,4},{9,1},{10,18},{11,15},{12,8... | collective-permute-start | bytes 1572872 | tf_op jit(solution)/shard_map/ppermute | solution.py:286
  18.0 16.4 %collective-permute-start = (bf16[8,128,256]{2,1,0:T(8,128)(2,1)S(1)}, bf16[8,128,256]{2,1,0:T(8,128)(2,1)S(1)}, u32[]{:S(2)}, u32[]{:S(2)}) collective-permute-start(bf16[8,128,256]{2,1,0:T(8,128)(2,1)S(1)} %get-tuple-element.18.own_ref.scaled_ref), channel_id=1, source_target_pairs={{0,8},{1,5},{4,12},{5,9},{6,2},{8,16},{9,13},{10,6},{11,3},{12,20}... | collective-permute-start | bytes 1572872 | tf_op jit(solution)/shard_map/ppermute | solution.py:286
  19.4 3.4 %copy-start.1 = (bf16[64,256,256]{2,1,0:T(8,128)(2,1)S(1)}, bf16[64,256,256]{2,1,0:T(8,128)(2,1)}, u32[]{:S(2)}) copy-start(bf16[64,256,256]{2,1,0:T(8,128)(2,1)} %tiles_ref.5) | copy-start | bytes 25165828
  25.3 11.8 %copy-start.5 = (bf16[8,128,256]{2,1,0:T(8,128)(2,1)}, bf16[8,128,256]{2,1,0:T(8,128)(2,1)S(1)}, u32[]{:S(2)}) copy-start(bf16[8,128,256]{2,1,0:T(8,128)(2,1)S(1)} %get-tuple-element.26.own_ref) | copy-start | bytes 1572868
  25.3 26.2 %copy-start.7 = (bf16[8,128,256]{2,1,0:T(8,128)(2,1)}, bf16[8,128,256]{2,1,0:T(8,128)(2,1)S(1)}, u32[]{:S(2)}) copy-start(bf16[8,128,256]{2,1,0:T(8,128)(2,1)S(1)} %get-tuple-element.32.back_ref) | copy-start | bytes 1572868
  25.3 4.4 %collective-permute-start.1 = (bf16[4,128,256]{2,1,0:T(8,128)(2,1)S(1)}, bf16[4,128,256]{2,1,0:T(8,128)(2,1)S(1)}, u32[]{:S(2)}, u32[]{:S(2)}) collective-permute-start(bf16[4,128,256]{2,1,0:T(8,128)(2,1)S(1)} %get-tuple-element.21), channel_id=1, source_target_pairs={{0,1},{1,0},{2,3},{3,2},{4,5},{5,4},{6,7},{7,6},{8,9},{9,8},{10,11... | collective-permute-start | bytes 786440 | tf_op jit(solution)/shard_map/ppermute | solution.py:277
  28.6 1.5 %collective-permute-start.2 = (bf16[4,128,256]{2,1,0:T(8,128)(2,1)S(1)}, bf16[4,128,256]{2,1,0:T(8,128)(2,1)S(1)}, u32[]{:S(2)}, u32[]{:S(2)}) collective-permute-start(bf16[4,128,256]{2,1,0:T(8,128)(2,1)S(1)} %get-tuple-element.22), channel_id=1, source_target_pairs={{0,1},{1,0},{2,3},{3,2},{4,5},{5,4},{6,7},{7,6},{8,9},{9,8},{10,11... | collective-permute-start | bytes 786440 | tf_op jit(solution)/shard_map/ppermute | solution.py:277
  30.2 19.0 %collective-permute-start.6 = (bf16[8,128,256]{2,1,0:T(8,128)(2,1)S(1)}, bf16[8,128,256]{2,1,0:T(8,128)(2,1)S(1)}, u32[]{:S(2)}, u32[]{:S(2)}) collective-permute-start(bf16[8,128,256]{2,1,0:T(8,128)(2,1)S(1)} %pass.1.refs_1_), channel_id=1, source_target_pairs={{0,2},{1,3},{2,0},{3,1},{4,6},{5,7},{6,4},{7,5},{8,10},{9,11},{10,... | collective-permute-start | bytes 1572872 | tf_op jit(solution)/shard_map/ppermute | solution.py:277
  34.5 14.7 %collective-permute-start.3 = (bf16[8,128,256]{2,1,0:T(8,128)(2,1)S(1)}, bf16[8,128,256]{2,1,0:T(8,128)(2,1)S(1)}, u32[]{:S(2)}, u32[]{:S(2)}) collective-permute-start(bf16[8,128,256]{2,1,0:T(8,128)(2,1)S(1)} %after.3), channel_id=1, source_target_pairs={{0,1},{1,0},{2,3},{3,2},{4,5},{5,4},{6,7},{7,6},{8,9},{9,8},{10,11... | collective-permute-start | bytes 1572872 | tf_op jit(solution)/shard_map/ppermute | solution.py:277
  37.2 12.0 %collective-permute-start.5 = (bf16[8,128,256]{2,1,0:T(8,128)(2,1)S(1)}, bf16[8,128,256]{2,1,0:T(8,128)(2,1)S(1)}, u32[]{:S(2)}, u32[]{:S(2)}) collective-permute-start(bf16[8,128,256]{2,1,0:T(8,128)(2,1)S(1)} %after.4), channel_id=1, source_target_pairs={{0,1},{1,0},{2,3},{3,2},{4,5},{5,4},{6,7},{7,6},{8,9},{9,8},{10,11... | collective-permute-start | bytes 1572872 | tf_op jit(solution)/shard_map/ppermute | solution.py:277
  51.5 3.2 %collective-permute-start.7 = (bf16[2,8,32,256]{3,2,1,0:T(8,128)(2,1)S(1)}, bf16[2,8,32,256]{3,2,1,0:T(8,128)(2,1)S(1)}, u32[]{:S(2)}, u32[]{:S(2)}) collective-permute-start(bf16[2,8,32,256]{3,2,1,0:T(8,128)(2,1)S(1)} %get-tuple-element.24), channel_id=1, source_target_pairs={{0,1},{1,0},{2,3},{3,2},{4,5},{5,4},{6,7},{7,6},{8,9},{9,8},{10,11... | collective-permute-start | bytes 786440 | tf_op jit(solution)/shard_map/ppermute | solution.py:277
  53.6 1.9 %collective-permute-start.9 = (bf16[8,128,256]{2,1,0:T(8,128)(2,1)S(1)}, bf16[8,128,256]{2,1,0:T(8,128)(2,1)S(1)}, u32[]{:S(2)}, u32[]{:S(2)}) collective-permute-start(bf16[8,128,256]{2,1,0:T(8,128)(2,1)S(1)} %get-tuple-element.28), channel_id=1, source_target_pairs={{0,1},{1,0},{2,3},{3,2},{4,5},{5,4},{6,7},{7,6},{8,9},{9,8},{10,11... | collective-permute-start | bytes 1572872 | tf_op jit(solution)/shard_map/ppermute | solution.py:277
  54.8 4.8 %collective-permute-start.8 = (bf16[8,32,256]{2,1,0:T(8,128)(2,1)S(1)}, bf16[8,32,256]{2,1,0:T(8,128)(2,1)S(1)}, u32[]{:S(2)}, u32[]{:S(2)}) collective-permute-start(bf16[8,32,256]{2,1,0:T(8,128)(2,1)S(1)} %fusion.ready_ref), channel_id=1, source_target_pairs={{0,2},{1,3},{2,0},{3,1},{4,6},{5,7},{6,4},{7,5},{8,10},{9,11},{10,... | collective-permute-start | bytes 393224 | tf_op jit(solution)/shard_map/ppermute | solution.py:277
  55.7 23.0 %collective-permute-start.10 = (bf16[8,128,256]{2,1,0:T(8,128)(2,1)S(1)}, bf16[8,128,256]{2,1,0:T(8,128)(2,1)S(1)}, u32[]{:S(2)}, u32[]{:S(2)}) collective-permute-start(bf16[8,128,256]{2,1,0:T(8,128)(2,1)S(1)} %whole.1), channel_id=1, source_target_pairs={{2,6},{3,11},{5,1},{6,10},{7,15},{8,0},{9,5},{10,14},{11,19},{12,4... | collective-permute-start | bytes 1572872 | tf_op jit(solution)/shard_map/ppermute | solution.py:286
  60.5 29.5 %copy-start.8 = (bf16[8,128,256]{2,1,0:T(8,128)(2,1)S(1)}, bf16[8,128,256]{2,1,0:T(8,128)(2,1)}, u32[]{:S(2)}) copy-start(bf16[8,128,256]{2,1,0:T(8,128)(2,1)} %copy-done.7) | copy-start | bytes 1572868
  60.5 18.1 %all-to-all-start = ((bf16[8,32,256]{2,1,0:T(8,128)(2,1)}), bf16[8,32,256]{2,1,0:T(8,128)(2,1)S(1)}, u32[]{:S(2)}, u32[]{:S(2)}) async-start(bf16[8,32,256]{2,1,0:T(8,128)(2,1)} %get-tuple-element.25), calls=%async_computation | async-start | bytes 262144 | tf_op jit(solution)/shard_map/all_to_all | solution.py:357
  70.6 8.0 %collective-permute-start.11 = (bf16[8,32,256]{2,1,0:T(8,128)(2,1)S(1)}, bf16[8,32,256]{2,1,0:T(8,128)(2,1)S(1)}, u32[]{:S(2)}, u32[]{:S(2)}) collective-permute-start(bf16[8,32,256]{2,1,0:T(8,128)(2,1)S(1)} %get-tuple-element.29.agg0), channel_id=1, source_target_pairs={{0,2},{1,3},{2,0},{3,1},{4,6},{5,7},{6,4},{7,5},{8,10},{9,11},{10,... | collective-permute-start | bytes 393224 | tf_op jit(solution)/shard_map/ppermute | solution.py:277
  78.6 1.0 copy-start.6
  79.8 4.1 %collective-permute-start.12 = (bf16[2,2,128,256]{3,2,1,0:T(8,128)(2,1)S(1)}, bf16[2,2,128,256]{3,2,1,0:T(8,128)(2,1)S(1)}, u32[]{:S(2)}, u32[]{:S(2)}) collective-permute-start(bf16[2,2,128,256]{3,2,1,0:T(8,128)(2,1)S(1)} %get-tuple-element.31), channel_id=1, source_target_pairs={{0,1},{1,0},{2,3},{3,2},{4,5},{5,4},{6,7},{7,6},{8,9},{9,8},{10,11... | collective-permute-start | bytes 786440 | tf_op jit(solution)/shard_map/ppermute | solution.py:277
  83.9 6.1 %collective-permute-start.13 = (bf16[2,128,256]{2,1,0:T(8,128)(2,1)S(1)}, bf16[2,128,256]{2,1,0:T(8,128)(2,1)S(1)}, u32[]{:S(2)}, u32[]{:S(2)}) collective-permute-start(bf16[2,128,256]{2,1,0:T(8,128)(2,1)S(1)} %fusion.1.refs_1_), channel_id=1, source_target_pairs={{0,2},{1,3},{2,0},{3,1},{4,6},{5,7},{6,4},{7,5},{8,10},{9,11},{10,... | collective-permute-start | bytes 393224 | tf_op jit(solution)/shard_map/ppermute | solution.py:277
  84.0 21.1 %collective-permute-start.14 = (bf16[2,8,32,256]{3,2,1,0:T(8,128)(2,1)S(1)}, bf16[2,8,32,256]{3,2,1,0:T(8,128)(2,1)S(1)}, u32[]{:S(2)}, u32[]{:S(2)}) collective-permute-start(bf16[2,8,32,256]{3,2,1,0:T(8,128)(2,1)S(1)} %pad_maximum_fusion), channel_id=1, source_target_pairs={{0,1},{1,0},{2,3},{3,2},{4,5},{5,4},{6,7},{7,6},{8,9},{9,8},{10,11... | collective-permute-start | bytes 786440 | tf_op jit(solution)/shard_map/ppermute | solution.py:277
  85.2 11.8 %all-to-all-start.1 = ((bf16[8,32,256]{2,1,0:T(8,128)(2,1)}), bf16[8,32,256]{2,1,0:T(8,128)(2,1)S(1)}, u32[]{:S(2)}, u32[]{:S(2)}) async-start(bf16[8,32,256]{2,1,0:T(8,128)(2,1)} %after.5), calls=%async_computation.1 | async-start | bytes 262144 | tf_op jit(solution)/shard_map/all_to_all | solution.py:373

commit v3 on v2

--- a/solution.py
+++ b/solution.py
@@ -11,9 +11,9 @@
 STEP = 8
 COST = {
     "degree": 10, "scale": 1, "backward": 10, "pass": 1, "forward": 10, "whole": 1,
-    "aggregate": 10, "gather": 1, "split": 1, "pack": 1, "grad": 5, "finish": 1, "after": 0,
+    "aggregate": 10, "gather": 1, "add": 1, "finish": 10, "weight_grad": 1, "after": 0,
 }
-OFFSETS = (-2, -1, 1, 2)
+OFFSETS = (-1, 1, 2, -2)
 f32 = jnp.float32
 bf16 = jnp.bfloat16
 VMEM = pl.BlockSpec(memory_space=pltpu.VMEM)
@@ -204,49 +204,18 @@
         out_ref[part] = total.astype(bf16)
 
 
-def split_kernel(place_ref, own_ref, far_ref, ready_ref, also_ref, keep_ref, send_ref):
-    for ref, at, part in ((keep_ref, 0, 0), (send_ref, 0, 1), (keep_ref, 1, 2), (send_ref, 1, 3)):
-        first = (place_ref[0] ^ part) * 2
-        for k in range(2):
-            total = own_ref[first + k].astype(f32) + far_ref[first + k].astype(f32)
-            ref[at, k] = total.astype(bf16)
-
-
-def grad_kernel(place_ref, keep_ref, got_ref, other_ref, back_ref, inv_ref, out_ref):
-    first = place_ref[0] * 2
-    for k in range(2):
-        inv = inv_ref[pl.ds(first + k, 1)]
-        summed = keep_ref[0, k].astype(f32) + got_ref[0, k].astype(f32)
-        summed = summed + other_ref[k].astype(f32)
-        out_ref[k] = (inv * (summed + back_ref[first + k].astype(f32))).astype(bf16)
-
-
-def pack_kernel(terms_ref, grad_ref, out_ref):
-    quarter = terms_ref.shape[1]
-    width = grad_ref.shape[1]
-    total = terms_ref[0].astype(f32)
-    for part in range(1, terms_ref.shape[0]):
-        total = total + terms_ref[part].astype(f32)
-    high = total.astype(bf16)
-    out_ref[:quarter] = high
-    out_ref[quarter : 2 * quarter] = (total - high.astype(f32)).astype(bf16)
-    for k in range(2):
-        at = 2 * quarter + k * width
-        out_ref[at : at + width] = grad_ref[k]
+def add_kernel(a_ref, b_ref, *refs):
+    for block in range(a_ref.shape[0]):
+        refs[-1][block] = (a_ref[block].astype(f32) + b_ref[block].astype(f32)).astype(bf16)
 
 
 def finish_kernel(
-    place_ref, packed_ref, agg0, agg2, agg13, weight_ref, out_ref, grad_ref, weight_grad_ref
+    place_ref, agg0, agg2, agg13, weight_ref, pair_ref, other_ref, back_ref, inv_ref,
+    out_ref, grad_ref,
 ):
-    parts = packed_ref.shape[0]
-    width = weight_ref.shape[0]
-    quarter = width // parts
-    blocks = out_ref.shape[0] // BLOCK
-    for part in range(parts):
-        high = packed_ref[part, :quarter].astype(f32)
-        low = packed_ref[part, quarter : 2 * quarter].astype(f32)
-        weight_grad_ref[part * quarter : (part + 1) * quarter] = high + low
+    blocks, quarter, _ = agg0.shape
     for block in range(blocks):
+        rows = slice(block * BLOCK, (block + 1) * BLOCK)
         total = None
         for part, agg in enumerate((agg0, agg13.at[0], agg2, agg13.at[1])):
             start = pl.multiple_of((place_ref[0] ^ part) * quarter, quarter)
@@ -254,10 +223,20 @@
                 agg[block], weight_ref[pl.ds(start, quarter)], TN, preferred_element_type=f32
             )
             total = product if total is None else total + product
-        out_ref[block * BLOCK : (block + 1) * BLOCK] = total.astype(bf16)
-        part, k = divmod(block, blocks // parts)
-        at = 2 * quarter + k * width
-        grad_ref[block * BLOCK : (block + 1) * BLOCK] = packed_ref[part, at : at + width].T
+        out_ref[rows] = total.astype(bf16)
+        summed = pair_ref[block].astype(f32) + other_ref[block].astype(f32)
+        grad = inv_ref[block : block + 1] * (summed + back_ref[block].astype(f32))
+        grad_ref[rows] = grad.astype(bf16).T
+
+
+def weight_grad_kernel(terms_ref, ready_ref, out_ref):
+    quarter = terms_ref.shape[1]
+    parts = out_ref.shape[0] // quarter
+    for part in range(parts):
+        total = terms_ref[part].astype(f32)
+        for at in range(part + parts, terms_ref.shape[0], parts):
+            total = total + terms_ref[at].astype(f32)
+        out_ref[part * quarter : (part + 1) * quarter] = total
 
 
 def per_device(feats, tiles, tile_rows, tile_cols, tile_count, weight, cotangent):
@@ -287,7 +266,7 @@
 
     rows = tile_rows - wide * blocks
     offset = tile_cols // blocks - wide
-    owner = jnp.where(offset < 0, offset + 2, offset + 1)
+    owner = sum(jnp.where(offset == OFFSETS[n], n, 0) for n in range(narrows))
     part = jnp.where(offset == 0, 0, 1 + (owner ^ me))
     slots = part * blocks + tile_cols % blocks
 
@@ -358,39 +337,24 @@
     agg2 = swap(agg, 2)
     agg13 = swap(jnp.stack([agg, agg2]), 1)
     (terms,) = call(
-        gather_kernel, [VMEM], [shape((nears, quarter, hidden), bf16)], name="gather"
+        gather_kernel, [VMEM], [shape((nears * narrows, quarter, hidden), bf16)], name="gather"
     )(terms)
 
-    z_keep, z_send = call(
-        split_kernel,
-        [SMEM] + [VMEM] * 2 + [HBM] * 2,
-        [shape((2, 2, width, BLOCK), bf16)] * 2,
-        name="split",
-    )(place, q_own, q_far, terms, agg2)
-    z_got = swap(z_send, 1)
-    z_pass = (z_keep[1].astype(f32) + z_got[1].astype(f32)).astype(bf16)
-    z_other = swap(z_pass, 2)
-    terms = lax.all_to_all(after(terms, z_pass), "near", 0, 0)
-    (grad,) = call(
-        grad_kernel, [SMEM] + [VMEM] * 5, [shape((2, width, BLOCK), bf16)], name="grad"
-    )(place, z_keep, z_got, z_other, back, inv)
-    (packed,) = call(
-        pack_kernel,
-        [VMEM] * 2,
-        [shape((2 * quarter + 2 * width, BLOCK), bf16)],
-        name="pack",
-    )(terms, grad)
-    packed = lax.all_gather(packed, "narrow")
-    out, feats_grad, weight_grad = call(
+    (z,) = call(
+        add_kernel, [VMEM] * 2 + [HBM] * 2, [shape(block_shape, bf16)], name="add"
+    )(q_own, q_far, terms, agg2)
+    (z_pair,) = call(add_kernel, [VMEM] * 2, [shape(block_shape, bf16)], name="add")(z, swap(z, 1))
+    z_other = swap(z_pair, 2)
+    terms = lax.all_to_all(after(terms, z_pair), ("near", "narrow"), 0, 0)
+    out, feats_grad = call(
         finish_kernel,
-        [SMEM] + [VMEM] * 5,
-        [
-            shape((nodes, hidden), bf16),
-            shape((nodes, width), bf16),
-            shape((width, hidden), f32),
-        ],
+        [SMEM] + [VMEM] * 8,
+        [shape((nodes, hidden), bf16), shape((nodes, width), bf16)],
         name="finish",
-    )(place, packed, agg, agg2, agg13, weight)
+    )(place, agg, agg2, agg13, weight, z_pair, z_other, back, inv)
+    (weight_grad,) = call(
+        weight_grad_kernel, [VMEM, HBM], [shape((width, hidden), f32)], name="weight_grad"
+    )(terms, out)
     return (out, feats_grad, weight_grad)
 
 

time: 108 us -> 112 us (1.037); the launches traced: 108 us -> 110 us
  starting transfers between devices: 30.8 us -> 43.7 us
  blocking collectives: 17.6 us -> 7.86 us
  waiting for transfers between devices: 37.6 us -> 33.4 us
  Pallas kernels: 11.4 us -> 13.6 us
  local copies, waits for them, and re-layouts: 7.83 us -> 9.05 us
    all_gather x1 -> x0, blocking collectives: 8.16 us -> none  [per_device(): packed = lax.all_gather(packed, 'narrow')]
    ppermute x12, starting transfers between devices: 11.9 us -> 19.9 us  [swap(): return lax.ppermute(x, 'narrow', [(i, i ^ by) for i in range(narrows)])]
    all_to_all x1, waiting for transfers between devices: 7.94 us -> 3.34 us  [per_device(): terms = lax.all_to_all(terms, 'far', 0, 0)]
    all_to_all x1, starting transfers between devices: 4.86 us -> 8.83 us  [per_device(): terms = lax.all_to_all(after(terms, z_pair), ('near', 'narrow'), 0, 0)]
    ppermute x3, starting transfers between devices: 3.91 us -> 7 us  [fetch(): return lax.ppermute(x, WIDE + ('narrow',), pairs)]
    ppermute x12, waiting for transfers between devices: 18.8 us -> 15.8 us  [swap(): return lax.ppermute(x, 'narrow', [(i, i ^ by) for i in range(narrows)])]
    ppermute x3, waiting for transfers between devices: 4.11 us -> 6.63 us  [fetch(): return lax.ppermute(x, WIDE + ('narrow',), pairs)]
    all_to_all x1, starting transfers between devices: 10.1 us -> 7.99 us  [per_device(): terms = lax.all_to_all(terms, 'far', 0, 0)]
  transfers between devices with their start and end apart: 17 -> 17, of which waited for: 10 -> 10; matrix products, arithmetic and copies ran while one was open for 0% -> 0% of each run, Pallas kernels for 4% -> 7%
where the time goes in v3:
time: 112 us; the launch traced here: 110 us
  starting transfers between devices  43.7 us (39%)
  waiting for transfers between devices  33.4 us (30%)
  Pallas kernels  13.6 us (12%)
  local copies, waits for them, and re-layouts  9.05 us (8%)
  blocking collectives  7.86 us (7%)
  between operations  1.55 us (1%)
    ppermute x12, starting transfers between devices, swap(): return lax.ppermute(x, 'narrow', [(i, i ^ by) for i in range(narrows)])  19.9 us
    ppermute x12, waiting for transfers between devices, swap(): return lax.ppermute(x, 'narrow', [(i, i ^ by) for i in range(narrows)])  15.8 us
    unnamed x22, local copies, waits for them, and re-layouts  9.05 us
    all_to_all x1, starting transfers between devices, per_device(): terms = lax.all_to_all(after(terms, z_pair), ('near', 'narrow'), 0, 0)  8.83 us
    all_to_all x1, starting transfers between devices, per_device(): terms = lax.all_to_all(terms, 'far', 0, 0)  7.99 us
    all_gather x1, blocking collectives, per_device(): lax.all_gather(degree_part, 'narrow')  7.86 us
    all_to_all x1, waiting for transfers between devices, per_device(): terms = lax.all_to_all(after(terms, z_pair), ('near', 'narrow'), 0, 0)  7.67 us
    ppermute x3, starting transfers between devices, fetch(): return lax.ppermute(x, WIDE + ('narrow',), pairs)  7 us
  transfers between devices with their start and end apart: 17, of which 10 were waited for; matrix products, arithmetic and copies ran while one was open for 0% of the time, Pallas kernels for 7%

profile of v3, /device:TPU:1, one launch (start us, length us, event | category | flops | bytes accessed | tf_op | source)
XLA Modules:
  0.0 109.9 jit_solution(12344050197460812839)
XLA Ops:
  1.3 0.7 broadcast_subtract_fusion.rows_ref
  1.9 3.4 %copy-done = bf16[64,256,256]{2,1,0:T(8,128)(2,1)S(1)} copy-done((bf16[64,256,256]{2,1,0:T(8,128)(2,1)S(1)}, bf16[64,256,256]{2,1,0:T(8,128)(2,1)}, u32[]{:S(2)}) %copy-start) | copy-done | bytes 8388632
  5.3 2.1 %degree.1 = f32[8,256]{1,0:T(8,128)S(1)} custom-call(s32[1]{0:T(128)S(6)} %copy.10.count_ref, s32[64]{0:T(128)S(1)} %broadcast_subtract_fusion.rows_ref, bf16[64,256,256]{2,1,0:T(8,128)(2,1)S(1)} %copy-done), custom_call_target="tpu_custom_call" | custom-call | flops 10000000000 | bytes 10000000 | tf_op jit(solution)/shard_map/degree/pallas_call | solution.py:273
  7.5 7.9 %all-gather = f32[32,256]{1,0:T(8,128)S(1)} all-gather(f32[8,256]{1,0:T(8,128)S(1)} %degree.1), channel_id=2, replica_groups=mesh['far'=8,'near'=8,'narrow'=4] {'narrow'}, dimensions={0}, use_global_device_ids=true | all-gather | bytes 40960 | tf_op jit(solution)/shard_map/all_gather | solution.py:287
  15.3 0.2 scale.1
  15.5 3.5 %collective-permute-start.4 = (bf16[8,128,256]{2,1,0:T(8,128)(2,1)S(1)}, bf16[8,128,256]{2,1,0:T(8,128)(2,1)S(1)}, u32[]{:S(2)}, u32[]{:S(2)}) collective-permute-start(bf16[8,128,256]{2,1,0:T(8,128)(2,1)S(1)} %get-tuple-element.18.own_ref.scaled_ref), channel_id=1, source_target_pairs={{1,9},{2,6},{5,13},{6,10},{7,3},{8,0},{9,17},{10,14},{11,7},{12,4}... | collective-permute-start | bytes 1572872 | tf_op jit(solution)/shard_map/ppermute | solution.py:265
  19.0 1.3 %collective-permute-start = (bf16[8,128,256]{2,1,0:T(8,128)(2,1)S(1)}, bf16[8,128,256]{2,1,0:T(8,128)(2,1)S(1)}, u32[]{:S(2)}, u32[]{:S(2)}) collective-permute-start(bf16[8,128,256]{2,1,0:T(8,128)(2,1)S(1)} %get-tuple-element.18.own_ref.scaled_ref), channel_id=1, source_target_pairs={{0,4},{3,11},{4,8},{5,1},{7,15},{8,12},{9,5},{10,2},{11,19},{12,16... | collective-permute-start | bytes 1572872 | tf_op jit(solution)/shard_map/ppermute | solution.py:265
  20.4 3.4 %copy-done.1 = bf16[64,256,256]{2,1,0:T(8,128)(2,1)S(1)} copy-done((bf16[64,256,256]{2,1,0:T(8,128)(2,1)S(1)}, bf16[64,256,256]{2,1,0:T(8,128)(2,1)}, u32[]{:S(2)}) %copy-start.1) | copy-done | bytes 8388632
  23.8 2.9 %backward.1 = (bf16[8,128,256]{2,1,0:T(8,128)(2,1)S(1)}, bf16[8,128,256]{2,1,0:T(8,128)(2,1)S(1)}, bf16[8,128,256]{2,1,0:T(8,128)(2,1)S(1)}, bf16[8,128,256]{2,1...) custom-call(s32[1]{0:T(128)S(6)} %copy.10.count_ref, ...), custom_call_target="tpu_custom_call" | custom-call | flops 10000000000 | bytes 10000000 | tf_op jit(solution)/shard_map/backward/pallas_call | solution.py:293
  26.7 0.0 copy-start.8
  26.7 0.1 collective-permute-start.1
  26.8 0.5 collective-permute-start.2
  27.3 1.0 collective-permute-done.1.a_ref
  28.3 0.4 collective-permute-done.2.b_ref
  28.7 0.1 pass.1.refs_1_
  28.8 3.1 %collective-permute-start.6 = (bf16[8,128,256]{2,1,0:T(8,128)(2,1)S(1)}, bf16[8,128,256]{2,1,0:T(8,128)(2,1)S(1)}, u32[]{:S(2)}, u32[]{:S(2)}) collective-permute-start(bf16[8,128,256]{2,1,0:T(8,128)(2,1)S(1)} %pass.1.refs_1_), channel_id=1, source_target_pairs={{0,2},{1,3},{2,0},{3,1},{4,6},{5,7},{6,4},{7,5},{8,10},{9,11},{10,... | collective-permute-start | bytes 1572872 | tf_op jit(solution)/shard_map/ppermute | solution.py:256
  31.9 6.6 %collective-permute-done.refs_0_.x0 = bf16[8,128,256]{2,1,0:T(8,128)(2,1)S(1)} collective-permute-done((bf16[8,128,256]{2,1,0:T(8,128)(2,1)S(1)}, bf16[8,128,256]{2,1,0:T(8,128)(2,1)S(1)}, u32[]{:S(2)}, u32[]{:S(2)}) %collective-permute-start) | collective-permute-done | bytes 524320 | tf_op jit(solution)/shard_map/ppermute | solution.py:265
  38.6 0.1 collective-permute-start.3
  38.8 0.6 collective-permute-start.5
  39.3 7.5 %collective-permute-done.6.ready_ref.other_ref = bf16[8,128,256]{2,1,0:T(8,128)(2,1)S(1)} collective-permute-done((bf16[8,128,256]{2,1,0:T(8,128)(2,1)S(1)}, bf16[8,128,256]{2,1,0:T(8,128)(2,1)S(1)}, u32[]{:S(2)}, u32[]{:S(2)}) %collective-permute-start.6) | collective-permute-done | bytes 524320 | tf_op jit(solution)/shard_map/ppermute | solution.py:256
  46.9 2.8 %forward.1 = (bf16[2,8,32,256]{3,2,1,0:T(8,128)(2,1)S(1)}, bf16[2,8,32,256]{3,2,1,0:T(8,128)(2,1)S(1)}) custom-call(s32[1]{0:T(128)} %bitcast.place_ref, s32[1]{0:T(128)S(6)} %copy.10.count_ref, s32[64]{0:T(128)S(1)} %broadcast_subtract_fusion.rows_ref, s32[64]{0:T(128)S(1)} %fusion.1.slots_ref, bf16[64,256,256]{2,1,0:T(8,128)(2,1)S(1)} %copy-done.1, ...), custom_call_target="tpu_custom_call" | custom-call | flops 10000000000 | bytes 10000000 | tf_op jit(solution)/shard_map/forward/pallas_call | solution.py:309
  49.7 0.1 collective-permute-start.7
  49.8 0.5 collective-permute-start.11
  50.3 1.0 collective-permute-done.7.got_ref
  51.4 2.4 %collective-permute-start.8 = (bf16[8,32,256]{2,1,0:T(8,128)(2,1)S(1)}, bf16[8,32,256]{2,1,0:T(8,128)(2,1)S(1)}, u32[]{:S(2)}, u32[]{:S(2)}) collective-permute-start(bf16[8,32,256]{2,1,0:T(8,128)(2,1)S(1)} %fusion.ready_ref), channel_id=1, source_target_pairs={{0,2},{1,3},{2,0},{3,1},{4,6},{5,7},{6,4},{7,5},{8,10},{9,11},{10,... | collective-permute-start | bytes 393224 | tf_op jit(solution)/shard_map/ppermute | solution.py:256
  53.8 0.2 whole.1
  54.0 2.2 %collective-permute-start.12 = (bf16[8,128,256]{2,1,0:T(8,128)(2,1)S(1)}, bf16[8,128,256]{2,1,0:T(8,128)(2,1)S(1)}, u32[]{:S(2)}, u32[]{:S(2)}) collective-permute-start(bf16[8,128,256]{2,1,0:T(8,128)(2,1)S(1)} %whole.1), channel_id=1, source_target_pairs={{1,5},{2,10},{4,0},{5,9},{6,14},{8,4},{9,13},{10,18},{11,3},{12,8}... | collective-permute-start | bytes 1572872 | tf_op jit(solution)/shard_map/ppermute | solution.py:265
  56.2 1.3 %collective-permute-done.8.other_ref = bf16[8,32,256]{2,1,0:T(8,128)(2,1)S(1)} collective-permute-done((bf16[8,32,256]{2,1,0:T(8,128)(2,1)S(1)}, bf16[8,32,256]{2,1,0:T(8,128)(2,1)S(1)}, u32[]{:S(2)}, u32[]{:S(2)}) %collective-permute-start.8) | collective-permute-done | bytes 131104 | tf_op jit(solution)/shard_map/ppermute | solution.py:256
  57.5 0.9 aggregate.1
  58.4 8.0 %all-to-all-start = ((bf16[8,32,256]{2,1,0:T(8,128)(2,1)}), bf16[8,32,256]{2,1,0:T(8,128)(2,1)S(1)}, u32[]{:S(2)}, u32[]{:S(2)}) async-start(bf16[8,32,256]{2,1,0:T(8,128)(2,1)} %get-tuple-element.29), calls=%async_computation | async-start | bytes 262144 | tf_op jit(solution)/shard_map/all_to_all | solution.py:336
  66.4 4.6 %collective-permute-start.9 = (bf16[8,32,256]{2,1,0:T(8,128)(2,1)S(1)}, bf16[8,32,256]{2,1,0:T(8,128)(2,1)S(1)}, u32[]{:S(2)}, u32[]{:S(2)}) collective-permute-start(bf16[8,32,256]{2,1,0:T(8,128)(2,1)S(1)} %get-tuple-element.25.agg0), channel_id=1, source_target_pairs={{0,2},{1,3},{2,0},{3,1},{4,6},{5,7},{6,4},{7,5},{8,10},{9,11},{10,... | collective-permute-start | bytes 393224 | tf_op jit(solution)/shard_map/ppermute | solution.py:256
  71.0 3.3 %all-to-all-done.terms_ref = bf16[8,32,256]{2,1,0:T(8,128)(2,1)S(1)} async-done(((bf16[8,32,256]{2,1,0:T(8,128)(2,1)}), bf16[8,32,256]{2,1,0:T(8,128)(2,1)S(1)}, u32[]{:S(2)}, u32[]{:S(2)}) %all-to-all-start) | async-done | bytes 131104 | tf_op jit(solution)/shard_map/all_to_all | solution.py:336
  74.4 0.1 gather.1.refs_0_
  74.4 0.0 copy-start.7
  74.5 1.0 copy-done.7
  75.5 0.1 add.62.a_ref
  75.6 7.4 %collective-permute-start.13 = (bf16[8,128,256]{2,1,0:T(8,128)(2,1)S(1)}, bf16[8,128,256]{2,1,0:T(8,128)(2,1)S(1)}, u32[]{:S(2)}, u32[]{:S(2)}) collective-permute-start(bf16[8,128,256]{2,1,0:T(8,128)(2,1)S(1)} %add.62.a_ref), channel_id=1, source_target_pairs={{0,1},{1,0},{2,3},{3,2},{4,5},{5,4},{6,7},{7,6},{8,9},{9,8},{10,11... | collective-permute-start | bytes 1572872 | tf_op jit(solution)/shard_map/ppermute | solution.py:256
  83.0 1.5 %collective-permute-done.13.b_ref = bf16[8,128,256]{2,1,0:T(8,128)(2,1)S(1)} collective-permute-done((bf16[8,128,256]{2,1,0:T(8,128)(2,1)S(1)}, bf16[8,128,256]{2,1,0:T(8,128)(2,1)S(1)}, u32[]{:S(2)}, u32[]{:S(2)}) %collective-permute-start.13) | collective-permute-done | bytes 524320 | tf_op jit(solution)/shard_map/ppermute | solution.py:256
  84.5 0.1 add.63.pair_ref.refs_1_
  84.6 0.1 collective-permute-start.14
  84.8 0.5 collective-permute-start.10
  85.2 0.8 after.5
  86.1 8.8 %all-to-all-start.1 = ((bf16[32,32,256]{2,1,0:T(8,128)(2,1)}), bf16[32,32,256]{2,1,0:T(8,128)(2,1)S(1)}, u32[]{:S(2)}, u32[]{:S(2)}) async-start(bf16[32,32,256]{2,1,0:T(8,128)(2,1)} %after.5), calls=%async_computation.1 | async-start | bytes 1048576 | tf_op jit(solution)/shard_map/all_to_all | solution.py:348
  94.9 3.0 %collective-permute-done.14.other_ref = bf16[8,128,256]{2,1,0:T(8,128)(2,1)S(1)} collective-permute-done((bf16[8,128,256]{2,1,0:T(8,128)(2,1)S(1)}, bf16[8,128,256]{2,1,0:T(8,128)(2,1)S(1)}, u32[]{:S(2)}, u32[]{:S(2)}) %collective-permute-start.14) | collective-permute-done | bytes 524320 | tf_op jit(solution)/shard_map/ppermute | solution.py:256
  97.9 2.4 %finish.1 = (bf16[2048,256]{1,0:T(8,128)(2,1)}, bf16[2048,128]{1,0:T(8,128)(2,1)}) custom-call(s32[1]{0:T(128)} %bitcast.place_ref, bf16[8,32,256]{2,1,0:T(8,128)(2,1)S(1)} %get-tuple-element.25.agg0, bf16[8,32,256]{2,1,0:T(8,128)(2,1)S(1)} %collective-permute-done.9.refs_1_.agg2, bf16[2,8,32,256]{3,2,1,0:T(8,128)(2,1)S(1)} %collective-permute-done.10.agg13, ...), custom_call_target="tpu_custom_call" | custom-call | flops 10000000000 | bytes 10000000 | tf_op jit(solution)/shard_map/finish/pallas_call | solution.py:349
  100.3 7.7 %all-to-all-done.1.terms_ref = bf16[32,32,256]{2,1,0:T(8,128)(2,1)S(1)} async-done(((bf16[32,32,256]{2,1,0:T(8,128)(2,1)}), bf16[32,32,256]{2,1,0:T(8,128)(2,1)S(1)}, u32[]{:S(2)}, u32[]{:S(2)}) %all-to-all-start.1) | async-done | bytes 524320 | tf_op jit(solution)/shard_map/all_to_all | solution.py:348
  108.0 1.2 %copy-done.5 = bf16[2048,256]{1,0:T(8,128)(2,1)S(1)} copy-done((bf16[2048,256]{1,0:T(8,128)(2,1)S(1)}, bf16[2048,256]{1,0:T(8,128)(2,1)}, u32[]{:S(2)}) %copy-start.5) | copy-done | bytes 1048600
  109.2 0.7 weight_grad.1
  (28 shorter events, 0.2 us)
Async XLA Ops:
  1.9 3.4 %copy-start = (bf16[64,256,256]{2,1,0:T(8,128)(2,1)S(1)}, bf16[64,256,256]{2,1,0:T(8,128)(2,1)}, u32[]{:S(2)}) copy-start(bf16[64,256,256]{2,1,0:T(8,128)(2,1)} %tiles_ref.5) | copy-start | bytes 25165828
  5.3 10.0 %copy-start.3 = (bf16[2048,128]{1,0:T(8,128)(2,1)S(1)}, bf16[2048,128]{1,0:T(8,128)(2,1)}, u32[]{:S(2)}) copy-start(bf16[2048,128]{1,0:T(8,128)(2,1)} %param.7) | copy-start | bytes 1572868
  5.3 15.0 %copy-start.10 = (s32[64]{0:T(128)S(1)}, s32[64]{0:T(128)}, u32[]{:S(2)}) copy-start(s32[64]{0:T(128)} %param.10) | copy-start | bytes 772
  5.3 15.0 %copy-start.2 = (bf16[2048,256]{1,0:T(8,128)(2,1)S(1)}, bf16[2048,256]{1,0:T(8,128)(2,1)}, u32[]{:S(2)}) copy-start(bf16[2048,256]{1,0:T(8,128)(2,1)} %param.13) | copy-start | bytes 3145732
  5.3 15.1 %copy-start.4 = (bf16[128,256]{1,0:T(8,128)(2,1)S(1)}, bf16[128,256]{1,0:T(8,128)(2,1)}, u32[]{:S(2)}) copy-start(bf16[128,256]{1,0:T(8,128)(2,1)} %weight_ref.3) | copy-start | bytes 196612
  15.5 23.2 %collective-permute-start.4 = (bf16[8,128,256]{2,1,0:T(8,128)(2,1)S(1)}, bf16[8,128,256]{2,1,0:T(8,128)(2,1)S(1)}, u32[]{:S(2)}, u32[]{:S(2)}) collective-permute-start(bf16[8,128,256]{2,1,0:T(8,128)(2,1)S(1)} %get-tuple-element.18.own_ref.scaled_ref), channel_id=1, source_target_pairs={{1,9},{2,6},{5,13},{6,10},{7,3},{8,0},{9,17},{10,14},{11,7},{12,4}... | collective-permute-start | bytes 1572872 | tf_op jit(solution)/shard_map/ppermute | solution.py:265
  19.0 19.5 %collective-permute-start = (bf16[8,128,256]{2,1,0:T(8,128)(2,1)S(1)}, bf16[8,128,256]{2,1,0:T(8,128)(2,1)S(1)}, u32[]{:S(2)}, u32[]{:S(2)}) collective-permute-start(bf16[8,128,256]{2,1,0:T(8,128)(2,1)S(1)} %get-tuple-element.18.own_ref.scaled_ref), channel_id=1, source_target_pairs={{0,4},{3,11},{4,8},{5,1},{7,15},{8,12},{9,5},{10,2},{11,19},{12,16... | collective-permute-start | bytes 1572872 | tf_op jit(solution)/shard_map/ppermute | solution.py:265
  20.4 3.4 %copy-start.1 = (bf16[64,256,256]{2,1,0:T(8,128)(2,1)S(1)}, bf16[64,256,256]{2,1,0:T(8,128)(2,1)}, u32[]{:S(2)}) copy-start(bf16[64,256,256]{2,1,0:T(8,128)(2,1)} %tiles_ref.5) | copy-start | bytes 25165828
  26.7 12.0 %copy-start.6 = (bf16[8,128,256]{2,1,0:T(8,128)(2,1)}, bf16[8,128,256]{2,1,0:T(8,128)(2,1)S(1)}, u32[]{:S(2)}) copy-start(bf16[8,128,256]{2,1,0:T(8,128)(2,1)S(1)} %get-tuple-element.26.a_ref) | copy-start | bytes 1572868
  26.7 23.0 %copy-start.8 = (bf16[8,128,256]{2,1,0:T(8,128)(2,1)}, bf16[8,128,256]{2,1,0:T(8,128)(2,1)S(1)}, u32[]{:S(2)}) copy-start(bf16[8,128,256]{2,1,0:T(8,128)(2,1)S(1)} %get-tuple-element.30.back_ref) | copy-start | bytes 1572868
  26.7 1.6 %collective-permute-start.1 = (bf16[4,128,256]{2,1,0:T(8,128)(2,1)S(1)}, bf16[4,128,256]{2,1,0:T(8,128)(2,1)S(1)}, u32[]{:S(2)}, u32[]{:S(2)}) collective-permute-start(bf16[4,128,256]{2,1,0:T(8,128)(2,1)S(1)} %get-tuple-element.21), channel_id=1, source_target_pairs={{0,1},{1,0},{2,3},{3,2},{4,5},{5,4},{6,7},{7,6},{8,9},{9,8},{10,11... | collective-permute-start | bytes 786440 | tf_op jit(solution)/shard_map/ppermute | solution.py:256
  26.8 1.9 %collective-permute-start.2 = (bf16[4,128,256]{2,1,0:T(8,128)(2,1)S(1)}, bf16[4,128,256]{2,1,0:T(8,128)(2,1)S(1)}, u32[]{:S(2)}, u32[]{:S(2)}) collective-permute-start(bf16[4,128,256]{2,1,0:T(8,128)(2,1)S(1)} %get-tuple-element.22), channel_id=1, source_target_pairs={{0,1},{1,0},{2,3},{3,2},{4,5},{5,4},{6,7},{7,6},{8,9},{9,8},{10,11... | collective-permute-start | bytes 786440 | tf_op jit(solution)/shard_map/ppermute | solution.py:256
  28.8 18.1 %collective-permute-start.6 = (bf16[8,128,256]{2,1,0:T(8,128)(2,1)S(1)}, bf16[8,128,256]{2,1,0:T(8,128)(2,1)S(1)}, u32[]{:S(2)}, u32[]{:S(2)}) collective-permute-start(bf16[8,128,256]{2,1,0:T(8,128)(2,1)S(1)} %pass.1.refs_1_), channel_id=1, source_target_pairs={{0,2},{1,3},{2,0},{3,1},{4,6},{5,7},{6,4},{7,5},{8,10},{9,11},{10,... | collective-permute-start | bytes 1572872 | tf_op jit(solution)/shard_map/ppermute | solution.py:256
  38.6 8.3 %collective-permute-start.3 = (bf16[8,128,256]{2,1,0:T(8,128)(2,1)S(1)}, bf16[8,128,256]{2,1,0:T(8,128)(2,1)S(1)}, u32[]{:S(2)}, u32[]{:S(2)}) collective-permute-start(bf16[8,128,256]{2,1,0:T(8,128)(2,1)S(1)} %after.3), channel_id=1, source_target_pairs={{0,1},{1,0},{2,3},{3,2},{4,5},{5,4},{6,7},{7,6},{8,9},{9,8},{10,11... | collective-permute-start | bytes 1572872 | tf_op jit(solution)/shard_map/ppermute | solution.py:256
  38.8 8.1 %collective-permute-start.5 = (bf16[8,128,256]{2,1,0:T(8,128)(2,1)S(1)}, bf16[8,128,256]{2,1,0:T(8,128)(2,1)S(1)}, u32[]{:S(2)}, u32[]{:S(2)}) collective-permute-start(bf16[8,128,256]{2,1,0:T(8,128)(2,1)S(1)} %after.4), channel_id=1, source_target_pairs={{0,1},{1,0},{2,3},{3,2},{4,5},{5,4},{6,7},{7,6},{8,9},{9,8},{10,11... | collective-permute-start | bytes 1572872 | tf_op jit(solution)/shard_map/ppermute | solution.py:256
  49.7 1.6 %collective-permute-start.7 = (bf16[2,8,32,256]{3,2,1,0:T(8,128)(2,1)S(1)}, bf16[2,8,32,256]{3,2,1,0:T(8,128)(2,1)S(1)}, u32[]{:S(2)}, u32[]{:S(2)}) collective-permute-start(bf16[2,8,32,256]{3,2,1,0:T(8,128)(2,1)S(1)} %get-tuple-element.24), channel_id=1, source_target_pairs={{0,1},{1,0},{2,3},{3,2},{4,5},{5,4},{6,7},{7,6},{8,9},{9,8},{10,11... | collective-permute-start | bytes 786440 | tf_op jit(solution)/shard_map/ppermute | solution.py:256
  49.8 4.0 %collective-permute-start.11 = (bf16[8,128,256]{2,1,0:T(8,128)(2,1)S(1)}, bf16[8,128,256]{2,1,0:T(8,128)(2,1)S(1)}, u32[]{:S(2)}, u32[]{:S(2)}) collective-permute-start(bf16[8,128,256]{2,1,0:T(8,128)(2,1)S(1)} %get-tuple-element.28), channel_id=1, source_target_pairs={{0,1},{1,0},{2,3},{3,2},{4,5},{5,4},{6,7},{7,6},{8,9},{9,8},{10,11... | collective-permute-start | bytes 1572872 | tf_op jit(solution)/shard_map/ppermute | solution.py:256
  51.4 6.1 %collective-permute-start.8 = (bf16[8,32,256]{2,1,0:T(8,128)(2,1)S(1)}, bf16[8,32,256]{2,1,0:T(8,128)(2,1)S(1)}, u32[]{:S(2)}, u32[]{:S(2)}) collective-permute-start(bf16[8,32,256]{2,1,0:T(8,128)(2,1)S(1)} %fusion.ready_ref), channel_id=1, source_target_pairs={{0,2},{1,3},{2,0},{3,1},{4,6},{5,7},{6,4},{7,5},{8,10},{9,11},{10,... | collective-permute-start | bytes 393224 | tf_op jit(solution)/shard_map/ppermute | solution.py:256
  54.0 20.5 %collective-permute-start.12 = (bf16[8,128,256]{2,1,0:T(8,128)(2,1)S(1)}, bf16[8,128,256]{2,1,0:T(8,128)(2,1)S(1)}, u32[]{:S(2)}, u32[]{:S(2)}) collective-permute-start(bf16[8,128,256]{2,1,0:T(8,128)(2,1)S(1)} %whole.1), channel_id=1, source_target_pairs={{1,5},{2,10},{4,0},{5,9},{6,14},{8,4},{9,13},{10,18},{11,3},{12,8}... | collective-permute-start | bytes 1572872 | tf_op jit(solution)/shard_map/ppermute | solution.py:265
  58.4 39.4 %copy-start.9 = (bf16[8,128,256]{2,1,0:T(8,128)(2,1)S(1)}, bf16[8,128,256]{2,1,0:T(8,128)(2,1)}, u32[]{:S(2)}) copy-start(bf16[8,128,256]{2,1,0:T(8,128)(2,1)} %copy-done.8) | copy-start | bytes 1572868
  58.4 15.9 %all-to-all-start = ((bf16[8,32,256]{2,1,0:T(8,128)(2,1)}), bf16[8,32,256]{2,1,0:T(8,128)(2,1)S(1)}, u32[]{:S(2)}, u32[]{:S(2)}) async-start(bf16[8,32,256]{2,1,0:T(8,128)(2,1)} %get-tuple-element.29), calls=%async_computation | async-start | bytes 262144 | tf_op jit(solution)/shard_map/all_to_all | solution.py:336
  66.4 8.0 %collective-permute-start.9 = (bf16[8,32,256]{2,1,0:T(8,128)(2,1)S(1)}, bf16[8,32,256]{2,1,0:T(8,128)(2,1)S(1)}, u32[]{:S(2)}, u32[]{:S(2)}) collective-permute-start(bf16[8,32,256]{2,1,0:T(8,128)(2,1)S(1)} %get-tuple-element.25.agg0), channel_id=1, source_target_pairs={{0,2},{1,3},{2,0},{3,1},{4,6},{5,7},{6,4},{7,5},{8,10},{9,11},{10,... | collective-permute-start | bytes 393224 | tf_op jit(solution)/shard_map/ppermute | solution.py:256
  74.4 1.0 copy-start.7
  75.6 8.9 %collective-permute-start.13 = (bf16[8,128,256]{2,1,0:T(8,128)(2,1)S(1)}, bf16[8,128,256]{2,1,0:T(8,128)(2,1)S(1)}, u32[]{:S(2)}, u32[]{:S(2)}) collective-permute-start(bf16[8,128,256]{2,1,0:T(8,128)(2,1)S(1)} %add.62.a_ref), channel_id=1, source_target_pairs={{0,1},{1,0},{2,3},{3,2},{4,5},{5,4},{6,7},{7,6},{8,9},{9,8},{10,11... | collective-permute-start | bytes 1572872 | tf_op jit(solution)/shard_map/ppermute | solution.py:256
  84.6 13.2 %collective-permute-start.14 = (bf16[8,128,256]{2,1,0:T(8,128)(2,1)S(1)}, bf16[8,128,256]{2,1,0:T(8,128)(2,1)S(1)}, u32[]{:S(2)}, u32[]{:S(2)}) collective-permute-start(bf16[8,128,256]{2,1,0:T(8,128)(2,1)S(1)} %add.63.pair_ref.refs_1_), channel_id=1, source_target_pairs={{0,2},{1,3},{2,0},{3,1},{4,6},{5,7},{6,4},{7,5},{8,10},{9,11},{10,... | collective-permute-start | bytes 1572872 | tf_op jit(solution)/shard_map/ppermute | solution.py:256
  84.8 10.1 %collective-permute-start.10 = (bf16[2,8,32,256]{3,2,1,0:T(8,128)(2,1)S(1)}, bf16[2,8,32,256]{3,2,1,0:T(8,128)(2,1)S(1)}, u32[]{:S(2)}, u32[]{:S(2)}) collective-permute-start(bf16[2,8,32,256]{3,2,1,0:T(8,128)(2,1)S(1)} %pad_maximum_fusion), channel_id=1, source_target_pairs={{0,1},{1,0},{2,3},{3,2},{4,5},{5,4},{6,7},{7,6},{8,9},{9,8},{10,11... | collective-permute-start | bytes 786440 | tf_op jit(solution)/shard_map/ppermute | solution.py:256
  86.1 21.9 %all-to-all-start.1 = ((bf16[32,32,256]{2,1,0:T(8,128)(2,1)}), bf16[32,32,256]{2,1,0:T(8,128)(2,1)S(1)}, u32[]{:S(2)}, u32[]{:S(2)}) async-start(bf16[32,32,256]{2,1,0:T(8,128)(2,1)} %after.5), calls=%async_computation.1 | async-start | bytes 1048576 | tf_op jit(solution)/shard_map/all_to_all | solution.py:348
  108.0 1.2 %copy-start.5 = (bf16[2048,256]{1,0:T(8,128)(2,1)S(1)}, bf16[2048,256]{1,0:T(8,128)(2,1)}, u32[]{:S(2)}) copy-start(bf16[2048,256]{1,0:T(8,128)(2,1)} %get-tuple-element.15.ready_ref) | copy-start | bytes 3145732

commit v4 on v3

--- a/solution.py
+++ b/solution.py
@@ -8,7 +8,7 @@
 WIDE = ("far", "near")
 BLOCK = 256
 REACH = 2
-STEP = 8
+STEP = 16
 COST = {
     "degree": 10, "scale": 1, "backward": 10, "pass": 1, "forward": 10, "whole": 1,
     "aggregate": 10, "gather": 1, "add": 1, "finish": 10, "weight_grad": 1, "after": 0,

time: 112 us -> 105 us (0.938)
  starting transfers between devices: 43.7 us -> 28.6 us
  waiting for transfers between devices: 33.4 us -> 41.4 us
  Pallas kernels: 13.6 us -> 14.8 us
    ppermute x12, starting transfers between devices: 19.9 us -> 9.68 us  [swap(): return lax.ppermute(x, 'narrow', [(i, i ^ by) for i in range(narrows)])]
    ppermute x3, waiting for transfers between devices: 6.63 us -> 11.1 us  [fetch(): return lax.ppermute(x, WIDE + ('narrow',), pairs)]
    all_to_all x1, starting transfers between devices: 8.83 us -> 4.67 us  [per_device(): terms = lax.all_to_all(after(terms, z_pair), ('near', 'narrow'), 0, 0)]
    ppermute x12, waiting for transfers between devices: 15.8 us -> 18.9 us  [swap(): return lax.ppermute(x, 'narrow', [(i, i ^ by) for i in range(narrows)])]
    all_to_all x1, waiting for transfers between devices: 3.34 us -> 6.3 us  [per_device(): terms = lax.all_to_all(terms, 'far', 0, 0)]
    all_to_all x1, waiting for transfers between devices: 7.67 us -> 5.16 us  [per_device(): terms = lax.all_to_all(after(terms, z_pair), ('near', 'narrow'), 0, 0)]
    ppermute x3, starting transfers between devices: 7 us -> 5.43 us  [fetch(): return lax.ppermute(x, WIDE + ('narrow',), pairs)]
  transfers between devices with their start and end apart: 17 -> 17, of which waited for: 10 -> 11; matrix products, arithmetic and copies ran while one was open for 0% -> 0% of each run, Pallas kernels for 7% -> 7%
where the time goes in v4:
time: 105 us; the launch traced here: 104 us
  waiting for transfers between devices  41.4 us (39%)
  starting transfers between devices  28.6 us (27%)
  Pallas kernels  14.8 us (14%)
  local copies, waits for them, and re-layouts  9.05 us (9%)
  blocking collectives  7.57 us (7%)
  between operations  1.55 us (1%)
    ppermute x12, waiting for transfers between devices, swap(): return lax.ppermute(x, 'narrow', [(i, i ^ by) for i in range(narrows)])  18.9 us
    ppermute x3, waiting for transfers between devices, fetch(): return lax.ppermute(x, WIDE + ('narrow',), pairs)  11.1 us
    ppermute x12, starting transfers between devices, swap(): return lax.ppermute(x, 'narrow', [(i, i ^ by) for i in range(narrows)])  9.68 us
    unnamed x22, local copies, waits for them, and re-layouts  9.05 us
    all_to_all x1, starting transfers between devices, per_device(): terms = lax.all_to_all(terms, 'far', 0, 0)  8.86 us
    all_gather x1, blocking collectives, per_device(): lax.all_gather(degree_part, 'narrow')  7.57 us
    all_to_all x1, waiting for transfers between devices, per_device(): terms = lax.all_to_all(terms, 'far', 0, 0)  6.3 us
    ppermute x3, starting transfers between devices, fetch(): return lax.ppermute(x, WIDE + ('narrow',), pairs)  5.43 us
  transfers between devices with their start and end apart: 17, of which 11 were waited for; matrix products, arithmetic and copies ran while one was open for 0% of the time, Pallas kernels for 7%

profile of v4, /device:TPU:1, one launch (start us, length us, event | category | flops | bytes accessed | tf_op | source)
XLA Modules:
  0.0 103.7 jit_solution(11132070705740462958)
XLA Ops:
  1.3 0.7 broadcast_subtract_fusion.rows_ref
  1.9 3.4 %copy-done = bf16[64,256,256]{2,1,0:T(8,128)(2,1)S(1)} copy-done((bf16[64,256,256]{2,1,0:T(8,128)(2,1)S(1)}, bf16[64,256,256]{2,1,0:T(8,128)(2,1)}, u32[]{:S(2)}) %copy-start) | copy-done | bytes 8388632
  5.3 2.6 %degree.1 = f32[8,256]{1,0:T(8,128)S(1)} custom-call(s32[1]{0:T(128)S(6)} %copy.10.count_ref, s32[64]{0:T(128)S(1)} %broadcast_subtract_fusion.rows_ref, bf16[64,256,256]{2,1,0:T(8,128)(2,1)S(1)} %copy-done), custom_call_target="tpu_custom_call" | custom-call | flops 10000000000 | bytes 10000000 | tf_op jit(solution)/shard_map/degree/pallas_call | solution.py:273
  7.9 7.6 %all-gather = f32[32,256]{1,0:T(8,128)S(1)} all-gather(f32[8,256]{1,0:T(8,128)S(1)} %degree.1), channel_id=2, replica_groups=mesh['far'=8,'near'=8,'narrow'=4] {'narrow'}, dimensions={0}, use_global_device_ids=true | all-gather | bytes 40960 | tf_op jit(solution)/shard_map/all_gather | solution.py:287
  15.5 0.2 scale.1
  15.7 2.8 %collective-permute-start.4 = (bf16[8,128,256]{2,1,0:T(8,128)(2,1)S(1)}, bf16[8,128,256]{2,1,0:T(8,128)(2,1)S(1)}, u32[]{:S(2)}, u32[]{:S(2)}) collective-permute-start(bf16[8,128,256]{2,1,0:T(8,128)(2,1)S(1)} %get-tuple-element.18.own_ref.scaled_ref), channel_id=1, source_target_pairs={{1,9},{2,6},{5,13},{6,10},{7,3},{8,0},{9,17},{10,14},{11,7},{12,4}... | collective-permute-start | bytes 1572872 | tf_op jit(solution)/shard_map/ppermute | solution.py:265
  18.5 1.3 %collective-permute-start = (bf16[8,128,256]{2,1,0:T(8,128)(2,1)S(1)}, bf16[8,128,256]{2,1,0:T(8,128)(2,1)S(1)}, u32[]{:S(2)}, u32[]{:S(2)}) collective-permute-start(bf16[8,128,256]{2,1,0:T(8,128)(2,1)S(1)} %get-tuple-element.18.own_ref.scaled_ref), channel_id=1, source_target_pairs={{0,4},{3,11},{4,8},{5,1},{7,15},{8,12},{9,5},{10,2},{11,19},{12,16... | collective-permute-start | bytes 1572872 | tf_op jit(solution)/shard_map/ppermute | solution.py:265
  19.9 0.0 copy-start.1
  19.9 3.4 %copy-done.1 = bf16[64,256,256]{2,1,0:T(8,128)(2,1)S(1)} copy-done((bf16[64,256,256]{2,1,0:T(8,128)(2,1)S(1)}, bf16[64,256,256]{2,1,0:T(8,128)(2,1)}, u32[]{:S(2)}) %copy-start.1) | copy-done | bytes 8388632
  23.2 3.1 %backward.1 = (bf16[8,128,256]{2,1,0:T(8,128)(2,1)S(1)}, bf16[8,128,256]{2,1,0:T(8,128)(2,1)S(1)}, bf16[8,128,256]{2,1,0:T(8,128)(2,1)S(1)}, bf16[8,128,256]{2,1...) custom-call(s32[1]{0:T(128)S(6)} %copy.10.count_ref, ...), custom_call_target="tpu_custom_call" | custom-call | flops 10000000000 | bytes 10000000 | tf_op jit(solution)/shard_map/backward/pallas_call | solution.py:293
  26.4 0.1 collective-permute-start.1
  26.5 0.5 collective-permute-start.2
  27.0 1.0 collective-permute-done.1.a_ref
  28.0 0.4 collective-permute-done.2.b_ref
  28.4 0.1 pass.1.refs_1_
  28.5 1.3 %collective-permute-start.6 = (bf16[8,128,256]{2,1,0:T(8,128)(2,1)S(1)}, bf16[8,128,256]{2,1,0:T(8,128)(2,1)S(1)}, u32[]{:S(2)}, u32[]{:S(2)}) collective-permute-start(bf16[8,128,256]{2,1,0:T(8,128)(2,1)S(1)} %pass.1.refs_1_), channel_id=1, source_target_pairs={{0,2},{1,3},{2,0},{3,1},{4,6},{5,7},{6,4},{7,5},{8,10},{9,11},{10,... | collective-permute-start | bytes 1572872 | tf_op jit(solution)/shard_map/ppermute | solution.py:256
  29.8 11.0 %collective-permute-done.refs_0_.x0 = bf16[8,128,256]{2,1,0:T(8,128)(2,1)S(1)} collective-permute-done((bf16[8,128,256]{2,1,0:T(8,128)(2,1)S(1)}, bf16[8,128,256]{2,1,0:T(8,128)(2,1)S(1)}, u32[]{:S(2)}, u32[]{:S(2)}) %collective-permute-start) | collective-permute-done | bytes 524320 | tf_op jit(solution)/shard_map/ppermute | solution.py:265
  40.9 0.1 collective-permute-start.3
  41.1 0.6 collective-permute-start.5
  41.7 5.9 %collective-permute-done.6.ready_ref.other_ref = bf16[8,128,256]{2,1,0:T(8,128)(2,1)S(1)} collective-permute-done((bf16[8,128,256]{2,1,0:T(8,128)(2,1)S(1)}, bf16[8,128,256]{2,1,0:T(8,128)(2,1)S(1)}, u32[]{:S(2)}, u32[]{:S(2)}) %collective-permute-start.6) | collective-permute-done | bytes 524320 | tf_op jit(solution)/shard_map/ppermute | solution.py:256
  47.6 3.3 %forward.1 = (bf16[2,8,32,256]{3,2,1,0:T(8,128)(2,1)S(1)}, bf16[2,8,32,256]{3,2,1,0:T(8,128)(2,1)S(1)}) custom-call(s32[1]{0:T(128)} %bitcast.place_ref, s32[1]{0:T(128)S(6)} %copy.10.count_ref, s32[64]{0:T(128)S(1)} %broadcast_subtract_fusion.rows_ref, s32[64]{0:T(128)S(1)} %fusion.1.slots_ref, bf16[64,256,256]{2,1,0:T(8,128)(2,1)S(1)} %copy-done.1, ...), custom_call_target="tpu_custom_call" | custom-call | flops 10000000000 | bytes 10000000 | tf_op jit(solution)/shard_map/forward/pallas_call | solution.py:309
  50.9 0.1 collective-permute-start.7
  51.0 0.5 collective-permute-start.11
  51.5 1.0 collective-permute-done.7.got_ref
  52.6 0.1 collective-permute-start.8
  52.7 0.6 collective-permute-done.11.got_ref
  53.3 0.2 whole.1
  53.5 1.3 %collective-permute-start.12 = (bf16[8,128,256]{2,1,0:T(8,128)(2,1)S(1)}, bf16[8,128,256]{2,1,0:T(8,128)(2,1)S(1)}, u32[]{:S(2)}, u32[]{:S(2)}) collective-permute-start(bf16[8,128,256]{2,1,0:T(8,128)(2,1)S(1)} %whole.1), channel_id=1, source_target_pairs={{1,5},{2,10},{4,0},{5,9},{6,14},{8,4},{9,13},{10,18},{11,3},{12,8}... | collective-permute-start | bytes 1572872 | tf_op jit(solution)/shard_map/ppermute | solution.py:265
  54.8 2.8 %collective-permute-done.8.other_ref = bf16[8,32,256]{2,1,0:T(8,128)(2,1)S(1)} collective-permute-done((bf16[8,32,256]{2,1,0:T(8,128)(2,1)S(1)}, bf16[8,32,256]{2,1,0:T(8,128)(2,1)S(1)}, u32[]{:S(2)}, u32[]{:S(2)}) %collective-permute-start.8) | collective-permute-done | bytes 131104 | tf_op jit(solution)/shard_map/ppermute | solution.py:256
  57.6 0.9 aggregate.1
  58.5 8.9 %all-to-all-start = ((bf16[8,32,256]{2,1,0:T(8,128)(2,1)}), bf16[8,32,256]{2,1,0:T(8,128)(2,1)S(1)}, u32[]{:S(2)}, u32[]{:S(2)}) async-start(bf16[8,32,256]{2,1,0:T(8,128)(2,1)} %get-tuple-element.29), calls=%async_computation | async-start | bytes 262144 | tf_op jit(solution)/shard_map/all_to_all | solution.py:336
  67.4 1.7 %collective-permute-start.9 = (bf16[8,32,256]{2,1,0:T(8,128)(2,1)S(1)}, bf16[8,32,256]{2,1,0:T(8,128)(2,1)S(1)}, u32[]{:S(2)}, u32[]{:S(2)}) collective-permute-start(bf16[8,32,256]{2,1,0:T(8,128)(2,1)S(1)} %get-tuple-element.25.agg0), channel_id=1, source_target_pairs={{0,2},{1,3},{2,0},{3,1},{4,6},{5,7},{6,4},{7,5},{8,10},{9,11},{10,... | collective-permute-start | bytes 393224 | tf_op jit(solution)/shard_map/ppermute | solution.py:256
  69.1 6.3 %all-to-all-done.terms_ref = bf16[8,32,256]{2,1,0:T(8,128)(2,1)S(1)} async-done(((bf16[8,32,256]{2,1,0:T(8,128)(2,1)}), bf16[8,32,256]{2,1,0:T(8,128)(2,1)S(1)}, u32[]{:S(2)}, u32[]{:S(2)}) %all-to-all-start) | async-done | bytes 131104 | tf_op jit(solution)/shard_map/all_to_all | solution.py:336
  75.4 0.1 gather.1.refs_0_
  75.5 1.0 copy-done.7
  76.6 0.1 add.62.a_ref
  76.7 2.6 %collective-permute-start.13 = (bf16[8,128,256]{2,1,0:T(8,128)(2,1)S(1)}, bf16[8,128,256]{2,1,0:T(8,128)(2,1)S(1)}, u32[]{:S(2)}, u32[]{:S(2)}) collective-permute-start(bf16[8,128,256]{2,1,0:T(8,128)(2,1)S(1)} %add.62.a_ref), channel_id=1, source_target_pairs={{0,1},{1,0},{2,3},{3,2},{4,5},{5,4},{6,7},{7,6},{8,9},{9,8},{10,11... | collective-permute-start | bytes 1572872 | tf_op jit(solution)/shard_map/ppermute | solution.py:256
  79.3 1.5 %collective-permute-done.13.b_ref = bf16[8,128,256]{2,1,0:T(8,128)(2,1)S(1)} collective-permute-done((bf16[8,128,256]{2,1,0:T(8,128)(2,1)S(1)}, bf16[8,128,256]{2,1,0:T(8,128)(2,1)S(1)}, u32[]{:S(2)}, u32[]{:S(2)}) %collective-permute-start.13) | collective-permute-done | bytes 524320 | tf_op jit(solution)/shard_map/ppermute | solution.py:256
  80.8 0.1 add.63.pair_ref.refs_1_
  80.9 1.3 %collective-permute-start.14 = (bf16[8,128,256]{2,1,0:T(8,128)(2,1)S(1)}, bf16[8,128,256]{2,1,0:T(8,128)(2,1)S(1)}, u32[]{:S(2)}, u32[]{:S(2)}) collective-permute-start(bf16[8,128,256]{2,1,0:T(8,128)(2,1)S(1)} %add.63.pair_ref.refs_1_), channel_id=1, source_target_pairs={{0,2},{1,3},{2,0},{3,1},{4,6},{5,7},{6,4},{7,5},{8,10},{9,11},{10,... | collective-permute-start | bytes 1572872 | tf_op jit(solution)/shard_map/ppermute | solution.py:256
  82.3 0.7 collective-permute-start.10
  83.0 0.8 after.5
  83.9 4.7 %all-to-all-start.1 = ((bf16[32,32,256]{2,1,0:T(8,128)(2,1)}), bf16[32,32,256]{2,1,0:T(8,128)(2,1)S(1)}, u32[]{:S(2)}, u32[]{:S(2)}) async-start(bf16[32,32,256]{2,1,0:T(8,128)(2,1)} %after.5), calls=%async_computation.1 | async-start | bytes 1048576 | tf_op jit(solution)/shard_map/all_to_all | solution.py:348
  88.6 5.6 %collective-permute-done.14.other_ref = bf16[8,128,256]{2,1,0:T(8,128)(2,1)S(1)} collective-permute-done((bf16[8,128,256]{2,1,0:T(8,128)(2,1)S(1)}, bf16[8,128,256]{2,1,0:T(8,128)(2,1)S(1)}, u32[]{:S(2)}, u32[]{:S(2)}) %collective-permute-start.14) | collective-permute-done | bytes 524320 | tf_op jit(solution)/shard_map/ppermute | solution.py:256
  94.2 2.4 %finish.1 = (bf16[2048,256]{1,0:T(8,128)(2,1)}, bf16[2048,128]{1,0:T(8,128)(2,1)}) custom-call(s32[1]{0:T(128)} %bitcast.place_ref, bf16[8,32,256]{2,1,0:T(8,128)(2,1)S(1)} %get-tuple-element.25.agg0, bf16[8,32,256]{2,1,0:T(8,128)(2,1)S(1)} %collective-permute-done.9.refs_1_.agg2, bf16[2,8,32,256]{3,2,1,0:T(8,128)(2,1)S(1)} %collective-permute-done.10.agg13, ...), custom_call_target="tpu_custom_call" | custom-call | flops 10000000000 | bytes 10000000 | tf_op jit(solution)/shard_map/finish/pallas_call | solution.py:349
  96.6 5.2 %all-to-all-done.1.terms_ref = bf16[32,32,256]{2,1,0:T(8,128)(2,1)S(1)} async-done(((bf16[32,32,256]{2,1,0:T(8,128)(2,1)}), bf16[32,32,256]{2,1,0:T(8,128)(2,1)S(1)}, u32[]{:S(2)}, u32[]{:S(2)}) %all-to-all-start.1) | async-done | bytes 524320 | tf_op jit(solution)/shard_map/all_to_all | solution.py:348
  101.8 1.2 %copy-done.5 = bf16[2048,256]{1,0:T(8,128)(2,1)S(1)} copy-done((bf16[2048,256]{1,0:T(8,128)(2,1)S(1)}, bf16[2048,256]{1,0:T(8,128)(2,1)}, u32[]{:S(2)}) %copy-start.5) | copy-done | bytes 1048600
  103.0 0.7 weight_grad.1
  (28 shorter events, 0.2 us)
Async XLA Ops:
  1.9 3.4 %copy-start = (bf16[64,256,256]{2,1,0:T(8,128)(2,1)S(1)}, bf16[64,256,256]{2,1,0:T(8,128)(2,1)}, u32[]{:S(2)}) copy-start(bf16[64,256,256]{2,1,0:T(8,128)(2,1)} %tiles_ref.5) | copy-start | bytes 25165828
  5.3 10.2 %copy-start.3 = (bf16[2048,128]{1,0:T(8,128)(2,1)S(1)}, bf16[2048,128]{1,0:T(8,128)(2,1)}, u32[]{:S(2)}) copy-start(bf16[2048,128]{1,0:T(8,128)(2,1)} %param.7) | copy-start | bytes 1572868
  5.3 14.5 %copy-start.10 = (s32[64]{0:T(128)S(1)}, s32[64]{0:T(128)}, u32[]{:S(2)}) copy-start(s32[64]{0:T(128)} %param.10) | copy-start | bytes 772
  5.3 14.5 %copy-start.2 = (bf16[2048,256]{1,0:T(8,128)(2,1)S(1)}, bf16[2048,256]{1,0:T(8,128)(2,1)}, u32[]{:S(2)}) copy-start(bf16[2048,256]{1,0:T(8,128)(2,1)} %param.13) | copy-start | bytes 3145732
  5.3 14.5 %copy-start.4 = (bf16[128,256]{1,0:T(8,128)(2,1)S(1)}, bf16[128,256]{1,0:T(8,128)(2,1)}, u32[]{:S(2)}) copy-start(bf16[128,256]{1,0:T(8,128)(2,1)} %weight_ref.3) | copy-start | bytes 196612
  15.7 25.4 %collective-permute-start.4 = (bf16[8,128,256]{2,1,0:T(8,128)(2,1)S(1)}, bf16[8,128,256]{2,1,0:T(8,128)(2,1)S(1)}, u32[]{:S(2)}, u32[]{:S(2)}) collective-permute-start(bf16[8,128,256]{2,1,0:T(8,128)(2,1)S(1)} %get-tuple-element.18.own_ref.scaled_ref), channel_id=1, source_target_pairs={{1,9},{2,6},{5,13},{6,10},{7,3},{8,0},{9,17},{10,14},{11,7},{12,4}... | collective-permute-start | bytes 1572872 | tf_op jit(solution)/shard_map/ppermute | solution.py:265
  18.5 22.4 %collective-permute-start = (bf16[8,128,256]{2,1,0:T(8,128)(2,1)S(1)}, bf16[8,128,256]{2,1,0:T(8,128)(2,1)S(1)}, u32[]{:S(2)}, u32[]{:S(2)}) collective-permute-start(bf16[8,128,256]{2,1,0:T(8,128)(2,1)S(1)} %get-tuple-element.18.own_ref.scaled_ref), channel_id=1, source_target_pairs={{0,4},{3,11},{4,8},{5,1},{7,15},{8,12},{9,5},{10,2},{11,19},{12,16... | collective-permute-start | bytes 1572872 | tf_op jit(solution)/shard_map/ppermute | solution.py:265
  19.9 3.4 %copy-start.1 = (bf16[64,256,256]{2,1,0:T(8,128)(2,1)S(1)}, bf16[64,256,256]{2,1,0:T(8,128)(2,1)}, u32[]{:S(2)}) copy-start(bf16[64,256,256]{2,1,0:T(8,128)(2,1)} %tiles_ref.5) | copy-start | bytes 25165828
  26.4 14.7 %copy-start.6 = (bf16[8,128,256]{2,1,0:T(8,128)(2,1)}, bf16[8,128,256]{2,1,0:T(8,128)(2,1)S(1)}, u32[]{:S(2)}) copy-start(bf16[8,128,256]{2,1,0:T(8,128)(2,1)S(1)} %get-tuple-element.26.a_ref) | copy-start | bytes 1572868
  26.4 24.5 %copy-start.8 = (bf16[8,128,256]{2,1,0:T(8,128)(2,1)}, bf16[8,128,256]{2,1,0:T(8,128)(2,1)S(1)}, u32[]{:S(2)}) copy-start(bf16[8,128,256]{2,1,0:T(8,128)(2,1)S(1)} %get-tuple-element.30.back_ref) | copy-start | bytes 1572868
  26.4 1.6 %collective-permute-start.1 = (bf16[4,128,256]{2,1,0:T(8,128)(2,1)S(1)}, bf16[4,128,256]{2,1,0:T(8,128)(2,1)S(1)}, u32[]{:S(2)}, u32[]{:S(2)}) collective-permute-start(bf16[4,128,256]{2,1,0:T(8,128)(2,1)S(1)} %get-tuple-element.21), channel_id=1, source_target_pairs={{0,1},{1,0},{2,3},{3,2},{4,5},{5,4},{6,7},{7,6},{8,9},{9,8},{10,11... | collective-permute-start | bytes 786440 | tf_op jit(solution)/shard_map/ppermute | solution.py:256
  26.5 1.9 %collective-permute-start.2 = (bf16[4,128,256]{2,1,0:T(8,128)(2,1)S(1)}, bf16[4,128,256]{2,1,0:T(8,128)(2,1)S(1)}, u32[]{:S(2)}, u32[]{:S(2)}) collective-permute-start(bf16[4,128,256]{2,1,0:T(8,128)(2,1)S(1)} %get-tuple-element.22), channel_id=1, source_target_pairs={{0,1},{1,0},{2,3},{3,2},{4,5},{5,4},{6,7},{7,6},{8,9},{9,8},{10,11... | collective-permute-start | bytes 786440 | tf_op jit(solution)/shard_map/ppermute | solution.py:256
  28.5 19.0 %collective-permute-start.6 = (bf16[8,128,256]{2,1,0:T(8,128)(2,1)S(1)}, bf16[8,128,256]{2,1,0:T(8,128)(2,1)S(1)}, u32[]{:S(2)}, u32[]{:S(2)}) collective-permute-start(bf16[8,128,256]{2,1,0:T(8,128)(2,1)S(1)} %pass.1.refs_1_), channel_id=1, source_target_pairs={{0,2},{1,3},{2,0},{3,1},{4,6},{5,7},{6,4},{7,5},{8,10},{9,11},{10,... | collective-permute-start | bytes 1572872 | tf_op jit(solution)/shard_map/ppermute | solution.py:256
  40.9 6.6 %collective-permute-start.3 = (bf16[8,128,256]{2,1,0:T(8,128)(2,1)S(1)}, bf16[8,128,256]{2,1,0:T(8,128)(2,1)S(1)}, u32[]{:S(2)}, u32[]{:S(2)}) collective-permute-start(bf16[8,128,256]{2,1,0:T(8,128)(2,1)S(1)} %after.3), channel_id=1, source_target_pairs={{0,1},{1,0},{2,3},{3,2},{4,5},{5,4},{6,7},{7,6},{8,9},{9,8},{10,11... | collective-permute-start | bytes 1572872 | tf_op jit(solution)/shard_map/ppermute | solution.py:256
  41.1 6.5 %collective-permute-start.5 = (bf16[8,128,256]{2,1,0:T(8,128)(2,1)S(1)}, bf16[8,128,256]{2,1,0:T(8,128)(2,1)S(1)}, u32[]{:S(2)}, u32[]{:S(2)}) collective-permute-start(bf16[8,128,256]{2,1,0:T(8,128)(2,1)S(1)} %after.4), channel_id=1, source_target_pairs={{0,1},{1,0},{2,3},{3,2},{4,5},{5,4},{6,7},{7,6},{8,9},{9,8},{10,11... | collective-permute-start | bytes 1572872 | tf_op jit(solution)/shard_map/ppermute | solution.py:256
  50.9 1.6 %collective-permute-start.7 = (bf16[2,8,32,256]{3,2,1,0:T(8,128)(2,1)S(1)}, bf16[2,8,32,256]{3,2,1,0:T(8,128)(2,1)S(1)}, u32[]{:S(2)}, u32[]{:S(2)}) collective-permute-start(bf16[2,8,32,256]{3,2,1,0:T(8,128)(2,1)S(1)} %get-tuple-element.24), channel_id=1, source_target_pairs={{0,1},{1,0},{2,3},{3,2},{4,5},{5,4},{6,7},{7,6},{8,9},{9,8},{10,11... | collective-permute-start | bytes 786440 | tf_op jit(solution)/shard_map/ppermute | solution.py:256
  51.0 2.3 %collective-permute-start.11 = (bf16[8,128,256]{2,1,0:T(8,128)(2,1)S(1)}, bf16[8,128,256]{2,1,0:T(8,128)(2,1)S(1)}, u32[]{:S(2)}, u32[]{:S(2)}) collective-permute-start(bf16[8,128,256]{2,1,0:T(8,128)(2,1)S(1)} %get-tuple-element.28), channel_id=1, source_target_pairs={{0,1},{1,0},{2,3},{3,2},{4,5},{5,4},{6,7},{7,6},{8,9},{9,8},{10,11... | collective-permute-start | bytes 1572872 | tf_op jit(solution)/shard_map/ppermute | solution.py:256
  52.6 5.0 %collective-permute-start.8 = (bf16[8,32,256]{2,1,0:T(8,128)(2,1)S(1)}, bf16[8,32,256]{2,1,0:T(8,128)(2,1)S(1)}, u32[]{:S(2)}, u32[]{:S(2)}) collective-permute-start(bf16[8,32,256]{2,1,0:T(8,128)(2,1)S(1)} %fusion.ready_ref), channel_id=1, source_target_pairs={{0,2},{1,3},{2,0},{3,1},{4,6},{5,7},{6,4},{7,5},{8,10},{9,11},{10,... | collective-permute-start | bytes 393224 | tf_op jit(solution)/shard_map/ppermute | solution.py:256
  53.5 22.1 %collective-permute-start.12 = (bf16[8,128,256]{2,1,0:T(8,128)(2,1)S(1)}, bf16[8,128,256]{2,1,0:T(8,128)(2,1)S(1)}, u32[]{:S(2)}, u32[]{:S(2)}) collective-permute-start(bf16[8,128,256]{2,1,0:T(8,128)(2,1)S(1)} %whole.1), channel_id=1, source_target_pairs={{1,5},{2,10},{4,0},{5,9},{6,14},{8,4},{9,13},{10,18},{11,3},{12,8}... | collective-permute-start | bytes 1572872 | tf_op jit(solution)/shard_map/ppermute | solution.py:265
  58.5 35.6 %copy-start.9 = (bf16[8,128,256]{2,1,0:T(8,128)(2,1)S(1)}, bf16[8,128,256]{2,1,0:T(8,128)(2,1)}, u32[]{:S(2)}) copy-start(bf16[8,128,256]{2,1,0:T(8,128)(2,1)} %copy-done.8) | copy-start | bytes 1572868
  58.5 16.9 %all-to-all-start = ((bf16[8,32,256]{2,1,0:T(8,128)(2,1)}), bf16[8,32,256]{2,1,0:T(8,128)(2,1)S(1)}, u32[]{:S(2)}, u32[]{:S(2)}) async-start(bf16[8,32,256]{2,1,0:T(8,128)(2,1)} %get-tuple-element.29), calls=%async_computation | async-start | bytes 262144 | tf_op jit(solution)/shard_map/all_to_all | solution.py:336
  67.4 8.1 %collective-permute-start.9 = (bf16[8,32,256]{2,1,0:T(8,128)(2,1)S(1)}, bf16[8,32,256]{2,1,0:T(8,128)(2,1)S(1)}, u32[]{:S(2)}, u32[]{:S(2)}) collective-permute-start(bf16[8,32,256]{2,1,0:T(8,128)(2,1)S(1)} %get-tuple-element.25.agg0), channel_id=1, source_target_pairs={{0,2},{1,3},{2,0},{3,1},{4,6},{5,7},{6,4},{7,5},{8,10},{9,11},{10,... | collective-permute-start | bytes 393224 | tf_op jit(solution)/shard_map/ppermute | solution.py:256
  75.5 1.0 %copy-start.7 = (bf16[8,128,256]{2,1,0:T(8,128)(2,1)S(1)}, bf16[8,128,256]{2,1,0:T(8,128)(2,1)}, u32[]{:S(2)}) copy-start(bf16[8,128,256]{2,1,0:T(8,128)(2,1)} %copy-done.6) | copy-start | bytes 1572868
  76.7 4.1 %collective-permute-start.13 = (bf16[8,128,256]{2,1,0:T(8,128)(2,1)S(1)}, bf16[8,128,256]{2,1,0:T(8,128)(2,1)S(1)}, u32[]{:S(2)}, u32[]{:S(2)}) collective-permute-start(bf16[8,128,256]{2,1,0:T(8,128)(2,1)S(1)} %add.62.a_ref), channel_id=1, source_target_pairs={{0,1},{1,0},{2,3},{3,2},{4,5},{5,4},{6,7},{7,6},{8,9},{9,8},{10,11... | collective-permute-start | bytes 1572872 | tf_op jit(solution)/shard_map/ppermute | solution.py:256
  80.9 13.2 %collective-permute-start.14 = (bf16[8,128,256]{2,1,0:T(8,128)(2,1)S(1)}, bf16[8,128,256]{2,1,0:T(8,128)(2,1)S(1)}, u32[]{:S(2)}, u32[]{:S(2)}) collective-permute-start(bf16[8,128,256]{2,1,0:T(8,128)(2,1)S(1)} %add.63.pair_ref.refs_1_), channel_id=1, source_target_pairs={{0,2},{1,3},{2,0},{3,1},{4,6},{5,7},{6,4},{7,5},{8,10},{9,11},{10,... | collective-permute-start | bytes 1572872 | tf_op jit(solution)/shard_map/ppermute | solution.py:256
  82.3 6.3 %collective-permute-start.10 = (bf16[2,8,32,256]{3,2,1,0:T(8,128)(2,1)S(1)}, bf16[2,8,32,256]{3,2,1,0:T(8,128)(2,1)S(1)}, u32[]{:S(2)}, u32[]{:S(2)}) collective-permute-start(bf16[2,8,32,256]{3,2,1,0:T(8,128)(2,1)S(1)} %pad_maximum_fusion), channel_id=1, source_target_pairs={{0,1},{1,0},{2,3},{3,2},{4,5},{5,4},{6,7},{7,6},{8,9},{9,8},{10,11... | collective-permute-start | bytes 786440 | tf_op jit(solution)/shard_map/ppermute | solution.py:256
  83.9 17.9 %all-to-all-start.1 = ((bf16[32,32,256]{2,1,0:T(8,128)(2,1)}), bf16[32,32,256]{2,1,0:T(8,128)(2,1)S(1)}, u32[]{:S(2)}, u32[]{:S(2)}) async-start(bf16[32,32,256]{2,1,0:T(8,128)(2,1)} %after.5), calls=%async_computation.1 | async-start | bytes 1048576 | tf_op jit(solution)/shard_map/all_to_all | solution.py:348
  101.8 1.2 %copy-start.5 = (bf16[2048,256]{1,0:T(8,128)(2,1)S(1)}, bf16[2048,256]{1,0:T(8,128)(2,1)}, u32[]{:S(2)}) copy-start(bf16[2048,256]{1,0:T(8,128)(2,1)} %get-tuple-element.15.ready_ref) | copy-start | bytes 3145732
